TPU v7x, 1024 devices: a whole 8x8x8 slice. The times are simulated.
1024 devices in a mesh: node: 64 (over z, y), grp: 16 (over x, core).
Axes of the slice: x: 8, y: 8, z: 8, core: 2. Of those that a mesh axis runs over, the one named last changes fastest.
Arguments:
- nbr_feats: float32 [524288, 512], P(('node', 'grp')), may hold values from -6 to 6
- tgt_feats: float32 [131072, 512], P(('node', 'grp')), may hold values from -6 to 6
- msg_weight: bfloat16 [512, 512], replicated, may hold values from -0.25 to 0.25
- comb_weight: bfloat16 [1024, 512], replicated, may hold values from -0.1875 to 0.1875
- head_gain: float32 [8, 512], replicated, may hold values from 0.3 to 600, as said below
- owners: int32 [131072, 8], P(('node', 'grp')), may hold values from 0 to 63, all different within a row; in each aligned block of 128 rows (0 to 127, 128 to 255, ...) at most 24 rows name the same one
- serve_rows: int32 [1024, 64, 24], P(('node', 'grp')), may hold values from 0 to 511
- importance: int32 [131072, 8], P(('node', 'grp')), may hold values from 1 to 32
- labels: int32 [131072], P('node'), may hold values from 0 to 7
- positives: int32 [131072], P('node'), may hold values from 0 to 2047
Outputs:
- loss: float32 [131072], P(('node', 'grp'))
- grad_msg: float32 [512, 512], P(None, 'grp')
- grad_comb: float32 [1024, 512], P(None, 'grp')
- grad_head: float32 [8, 512], P(None, 'grp')
Inputs may be any that keep to these rules, and one draw needn't show every extreme that they name: `owners`: the 8 entries of one target differ. Among the 128 targets of one device no node index is named by more than 24 targets, and some node index is named by exactly 24 targets of some device. `head_gain`: Positive.
All inputs are finite; a program needn't handle non-finite values.
Results may differ from a plain program's by a relative error of at most 0.018.
The roundings to bfloat16 on the way count: a program that leaves them out, or rounds other values in their place, can miss the bound.
Values may be sent and summed in bfloat16 or wider, within the bound.
A program may use at most 64 MiB of HBM per device.

v0:
```python
import jax
import jax.numpy as jnp
from jax import lax
from jax.sharding import PartitionSpec as P

eps = 1e-05


def silu_slope(value):
    logistic = jax.nn.sigmoid(value)
    return logistic * (1.0 + value * (1.0 - logistic))


def contract_rows(left, right):
    return lax.dot_general(
        left, right, (((0,), (0,)), ((), ())), preferred_element_type=jnp.float32
    )


def contract_cols(left, right):
    return lax.dot_general(
        left, right, (((1,), (1,)), ((), ())), preferred_element_type=jnp.float32
    )


def softmax_terms(scores, picked, scale_rows):
    top_value = jnp.max(scores, axis=1, keepdims=True)
    exp_terms = jnp.exp(scores - top_value)
    totals = jnp.sum(exp_terms, axis=1, keepdims=True)
    log_total = top_value[:, 0] + jnp.log(totals[:, 0])
    column_ids = lax.broadcasted_iota(jnp.int32, scores.shape, 1)
    hit_mask = (column_ids == picked[:, None]).astype(jnp.float32)
    picked_score = jnp.sum(scores * hit_mask, axis=1)
    loss_rows = log_total - picked_score
    grad_scores = (exp_terms / totals - hit_mask) / scale_rows
    return (loss_rows, grad_scores)


def body(
    nbr_feats,
    tgt_feats,
    msg_weight,
    comb_weight,
    head_gain,
    owners,
    serve_rows,
    importance,
    labels,
    positives,
):
    feat_width = nbr_feats.shape[1]
    tgt_count = tgt_feats.shape[0]
    node_count = lax.axis_size("node")
    grp_count = lax.axis_size("grp")
    grp_rank = lax.axis_index("grp")
    group_rows = tgt_count * grp_count
    task_count = head_gain.shape[0]
    nbr_bf = nbr_feats.astype(jnp.bfloat16)
    msg_pre = jnp.dot(nbr_bf, msg_weight, preferred_element_type=jnp.float32)
    messages = jax.nn.silu(msg_pre).astype(jnp.bfloat16)
    served = serve_rows[0]
    capacity = served.shape[1]
    served_flat = served.reshape(-1)
    outgoing = jnp.take(messages, served_flat, axis=0).reshape(node_count, capacity, feat_width)
    incoming = lax.all_to_all(outgoing, "node", split_axis=0, concat_axis=0, tiled=True)
    neighbours = owners.shape[1]
    owner_flat = owners.reshape(-1)
    owner_hits = (owner_flat[:, None] == jnp.arange(node_count, dtype=jnp.int32)[None, :]).astype(
        jnp.int32
    )
    earlier = jnp.cumsum(owner_hits, axis=0) - owner_hits
    slot_index = jnp.sum(earlier * owner_hits, axis=1)
    slot_flat = owner_flat * capacity + slot_index
    received = jnp.take(incoming.reshape(node_count * capacity, feat_width), slot_flat, axis=0)
    received = received.reshape(tgt_count, neighbours, feat_width).astype(jnp.float32)
    weight_f = importance.astype(jnp.float32)
    weight_total = jnp.sum(weight_f, axis=1)
    aggregate = jnp.sum(weight_f[:, :, None] * received, axis=1) / weight_total[:, None]
    comb_in = jnp.concatenate(
        [tgt_feats.astype(jnp.bfloat16), aggregate.astype(jnp.bfloat16)], axis=1
    )
    comb_pre = jnp.dot(comb_in, comb_weight, preferred_element_type=jnp.float32)
    hidden = jax.nn.silu(comb_pre)
    inv_norm = lax.rsqrt(jnp.mean(hidden * hidden, axis=1) + eps)
    embed = (hidden * inv_norm[:, None]).astype(jnp.bfloat16)
    group_embed = lax.all_gather(embed, "grp", axis=0, tiled=True)
    task_hits = (labels[:, None] == jnp.arange(task_count, dtype=jnp.int32)[None, :]).astype(
        jnp.float32
    )
    group_gain = jnp.dot(task_hits, head_gain, precision=lax.Precision.HIGHEST)
    group_query = (group_embed.astype(jnp.float32) * group_gain).astype(jnp.bfloat16)
    row_start = grp_rank * tgt_count
    own_gain = lax.dynamic_slice_in_dim(group_gain, row_start, tgt_count, 0)
    own_query = lax.dynamic_slice_in_dim(group_query, row_start, tgt_count, 0)
    own_hits = lax.dynamic_slice_in_dim(task_hits, row_start, tgt_count, 0)
    own_pos = lax.dynamic_slice_in_dim(positives, row_start, tgt_count, 0)
    scores = contract_cols(own_query, group_embed) / feat_width
    loss_rows, grad_scores = softmax_terms(scores, own_pos, group_rows)
    grad_bf = (grad_scores / feat_width).astype(jnp.bfloat16)
    column_grad = lax.psum_scatter(
        contract_rows(grad_bf, own_query), "grp", scatter_dimension=0, tiled=True
    )
    query_grad = jnp.dot(grad_bf, group_embed, preferred_element_type=jnp.float32)
    embed_f = embed.astype(jnp.float32)
    head_part = lax.dot_general(
        own_hits, query_grad * embed_f, (((0,), (0,)), ((), ())), precision=lax.Precision.HIGHEST
    )
    embed_grad = query_grad * own_gain + column_grad
    inner = jnp.sum(hidden * embed_grad, axis=1)
    cube = inv_norm * inv_norm * inv_norm
    hidden_grad = inv_norm[:, None] * embed_grad - hidden * (cube * inner / feat_width)[:, None]
    pre_grad = (silu_slope(comb_pre) * hidden_grad).astype(jnp.bfloat16)
    comb_part = contract_rows(comb_in, pre_grad)
    agg_grad = contract_cols(pre_grad, comb_weight[feat_width:])
    share = weight_f / weight_total[:, None]
    msg_grad = (share[:, :, None] * agg_grad[:, None, :]).astype(jnp.bfloat16)
    returning = (
        jnp.zeros((node_count * capacity, feat_width), jnp.bfloat16)
        .at[slot_flat]
        .set(msg_grad.reshape(-1, feat_width))
    )
    arriving = lax.all_to_all(
        returning.reshape(node_count, capacity, feat_width),
        "node",
        split_axis=0,
        concat_axis=0,
        tiled=True,
    )
    row_grad = (
        jnp.zeros(msg_pre.shape, jnp.float32)
        .at[served_flat]
        .add(arriving.reshape(-1, feat_width).astype(jnp.float32))
    )
    msg_pre_grad = (silu_slope(msg_pre) * row_grad).astype(jnp.bfloat16)
    msg_part = contract_rows(nbr_bf, msg_pre_grad)
    shares = (
        lax.psum_scatter(
            msg_part.astype(jnp.bfloat16), "grp", scatter_dimension=1, tiled=True
        ).astype(jnp.float32),
        lax.psum_scatter(
            comb_part.astype(jnp.bfloat16), "grp", scatter_dimension=1, tiled=True
        ).astype(jnp.float32),
        lax.psum_scatter(
            head_part.astype(jnp.bfloat16), "grp", scatter_dimension=1, tiled=True
        ).astype(jnp.float32),
    )
    grad_msg, grad_comb, grad_head = lax.psum((shares[0], shares[1], shares[2]), "node")
    return (loss_rows, grad_msg, grad_comb, grad_head)


def solution(mesh):
    placed = (
        P(("node", "grp"), None),
        P(("node", "grp"), None),
        P(),
        P(),
        P(),
        P(("node", "grp"), None),
        P(("node", "grp"), None, None),
        P(("node", "grp"), None),
        P("node"),
        P("node"),
    )
    return jax.shard_map(
        body,
        mesh=mesh,
        in_specs=placed,
        out_specs=(P(("node", "grp")), P(None, "grp"), P(None, "grp"), P(None, "grp")),
        check_vma=False,
    )
```

profile of v0, /device:TPU:8, one launch (start us, length us, event | category | flops | bytes accessed | tf_op | source)
XLA Modules:
  0.0 709.7 jit_solution(2155805529799698799)
XLA Ops:
  7.2 0.8 copy.49
  8.0 0.7 compare_and_fusion
  8.7 0.1 reshape_squeeze.6
  8.9 0.1 copy.48
  9.0 2.7 multiply_convert_fusion.2
  11.7 4.8 gather_fusion
  16.5 1.4 broadcast_select_fusion
  17.9 23.5 %all-to-all-start = ((bf16[64,24,512]{2,1,0:T(8,128)(2,1)}), bf16[64,24,512]{2,1,0:T(8,128)(2,1)S(1)}, u32[]{:S(2)}, u32[]{:S(2)}) async-start(bf16[64,24,512]{2,1,0:T(8,128)(2,1)} %broadcast_select_fusion), calls=%async_computation | async-start | bytes 3145728 | tf_op jit(solution)/shard_map/all_to_all | solution.py:65
  41.5 0.0 all-gather.2.cloned.1.call-start
  41.6 0.1 copy.42
  41.7 0.1 eq.47
  41.8 0.1 reshape.145
  41.9 0.1 copy.50
  42.0 0.1 mul.143
  42.1 18.0 %reduce-window.6 = s32[64,8,128]{2,1,0:T(8,128)S(1)} reduce-window(s32[64,8,128]{2,1,0:T(8,128)S(1)} %fusion.22, s32[]{:T(128)} %constant.27.clone.1), window={size=1x1x128 pad=0_0x0_0x127_0}, to_apply=%region_0.1 | reduce-window | flops 8323072 | bytes 524292 | tf_op jit(solution)/shard_map/reduce-window
  60.1 0.1 slice.16
  60.2 0.1 copy.44
  60.4 0.1 copy.45
  60.5 0.1 copy.41
  60.6 0.1 broadcast_add_fusion
  60.8 0.1 fusion.15
  60.8 0.1 reduce_sum.68
  61.0 0.1 copy.47
  61.2 21.5 %all-to-all-done = bf16[64,24,512]{2,1,0:T(8,128)(2,1)S(1)} async-done(((bf16[64,24,512]{2,1,0:T(8,128)(2,1)}), bf16[64,24,512]{2,1,0:T(8,128)(2,1)S(1)}, u32[]{:S(2)}, u32[]{:S(2)}) %all-to-all-start) | async-done | bytes 1572896 | tf_op jit(solution)/shard_map/all_to_all | solution.py:65
  82.8 4.0 gather_fusion.1
  86.7 0.8 multiply_reduce_fusion
  87.6 0.1 divide_convert_fusion
  87.7 1.7 multiply_reduce_fusion.2
  89.3 0.8 multiply_convert_fusion.6
  90.1 0.0 all-gather.2.cloned.1.call-update
  90.1 0.0 reduce-scatter.7.cloned.1.call-start
  90.2 0.8 dynamic_slice.13
  91.0 3.4 fusion.25
  94.3 33.7 %all-gather.2.cloned.1.call-done = bf16[2048,512]{1,0:T(8,128)(2,1)} async-done(((bf16[128,512]{1,0:T(8,128)(2,1)}), bf16[2048,512]{1,0:T(8,128)(2,1)}) %all-gather.2.cloned.1.call-update) | async-done | bytes 2097168 | tf_op jit(solution)/shard_map/all_gather | solution.py:86
  128.0 1.0 multiply_convert_fusion.5
  129.0 2.5 fusion.35
  131.5 0.4 fusion.8
  131.9 2.9 fusion.33
  134.9 0.0 reduce-scatter.7.cloned.1.call-update
  134.9 0.1 copy.52
  135.0 0.1 mul.154
  135.1 67.2 %reduce-scatter.7.cloned.1.call-done = f32[128,512]{1,0:T(8,128)} async-done(((f32[2048,512]{1,0:T(8,128)}), f32[128,512]{1,0:T(8,128)}) %reduce-scatter.7.cloned.1.call-update) | async-done | bytes 262160 | tf_op jit(solution)/shard_map/reduce_scatter | solution.py:100
  202.3 2.4 multiply_reduce_fusion.1
  204.8 0.3 fusion.10
  205.1 6.8 scatter_custom_fusion
  211.9 14.4 %all-to-all-start.1 = ((bf16[64,24,512]{2,1,0:T(8,128)(2,1)}), bf16[64,24,512]{2,1,0:T(8,128)(2,1)S(1)}, u32[]{:S(2)}, u32[]{:S(2)}) async-start(bf16[64,24,512]{2,1,0:T(8,128)(2,1)} %bitcast.51), calls=%async_computation.2 | async-start | bytes 3145728 | tf_op jit(solution)/shard_map/all_to_all | solution.py:122
  226.3 0.0 reduce-scatter.13.cloned.1.call-start
  226.4 0.3 iota_compare_fusion.1
  226.7 0.2 convolution_convert_fusion.2
  227.0 0.8 copy.55
  227.8 0.0 reduce-scatter.13.cloned.1.call-update
  227.8 0.0 reduce-scatter.11.cloned.1.call-start
  227.8 2.5 convolution_convert_fusion
  230.3 0.0 reduce-scatter.11.cloned.1.call-update
  230.3 0.0 reduce-scatter.9.cloned.1.call-start
  230.4 36.8 %all-to-all-done.1 = bf16[64,24,512]{2,1,0:T(8,128)(2,1)S(1)} async-done(((bf16[64,24,512]{2,1,0:T(8,128)(2,1)}), bf16[64,24,512]{2,1,0:T(8,128)(2,1)S(1)}, u32[]{:S(2)}, u32[]{:S(2)}) %all-to-all-start.1) | async-done | bytes 1572896 | tf_op jit(solution)/shard_map/all_to_all | solution.py:122
  267.2 10.0 %scatter_custom_fusion.1 = f32[512,512]{1,0:T(8,128)S(1)} fusion(s32[1536]{0:T(1024)S(1)} %fusion.26, bf16[1536,512]{1,0:T(8,128)(2,1)S(1)} %bitcast.50, f32[]{:T(128)} %constant.41.clone.1), kind=kCustom, calls=%fused_computation.4 | custom fusion | flops 1572864 | bytes 2621444 | tf_op jit(solution)/shard_map/scatter-add | solution.py:132
  277.3 3.0 fusion.3
  280.3 0.5 add_subtract_fusion
  280.8 9.7 %reduce-scatter.13.cloned.1.call-done = bf16[32,8]{1,0:T(8,128)(2,1)} async-done(((bf16[512,8]{1,0:T(8,128)(2,1)}), bf16[32,8]{1,0:T(8,128)(2,1)}) %reduce-scatter.13.cloned.1.call-update) | async-done | bytes 528
  290.6 0.8 copy.56
  291.3 64.7 %reduce-scatter.11.cloned.1.call-done = bf16[1024,32]{0,1:T(8,128)(2,1)} async-done(((bf16[1024,512]{0,1:T(8,128)(2,1)}), bf16[1024,32]{0,1:T(8,128)(2,1)}) %reduce-scatter.11.cloned.1.call-update) | async-done | bytes 65552 | tf_op jit(solution)/shard_map/reduce_scatter | solution.py:140
  356.0 64.4 %reduce-scatter.9.cloned.1.call-done = bf16[512,32]{0,1:T(8,128)(2,1)} async-done(((bf16[512,512]{0,1:T(8,128)(2,1)}), bf16[512,32]{0,1:T(8,128)(2,1)}) %reduce-scatter.9.cloned.1.call-update) | async-done | bytes 32784 | tf_op jit(solution)/shard_map/reduce_scatter | solution.py:137
  420.4 282.8 %all-reduce.2 = (f32[512,32]{0,1:T(8,128)}, f32[1024,32]{0,1:T(8,128)}, f32[8,32]{1,0:T(8,128)}) all-reduce(bf16[512,32]{0,1:T(8,128)(2,1)} %reduce-scatter.9.cloned.1.call-done, bf16[1024,32]{0,1:T(8,128)(2,1)} %reduce-scatter.11.cloned.1.call-done, bf16[8,32]{1,0:T(8,128)(2,1)S(1)} %copy.56), channel_id=1, replica_groups=mesh['node'=64,'grp'=16] {'node'}, use_global_device_ids=true, to_apply=%region_14.15 | all-reduce | flops 49408 | bytes 296448 | tf_op jit(solution)/shard_map/psum | solution.py:147
  (35 shorter events, 0.3 us)
Async XLA Ops:
  7.2 1.8 copy-start
  17.9 23.6 %copy-start.3 = (s32[128,8]{0,1:T(8,128)S(1)}, s32[128,8]{0,1:T(8,128)}, u32[]{:S(2)}) copy-start(s32[128,8]{0,1:T(8,128)} %param.15) | copy-start | bytes 12292
  17.9 42.6 %copy-start.4 = (s32[128,8]{0,1:T(8,128)S(1)}, s32[128,8]{0,1:T(8,128)}, u32[]{:S(2)}) copy-start(s32[128,8]{0,1:T(8,128)} %param.17) | copy-start | bytes 12292
  17.9 64.8 %all-to-all-start = ((bf16[64,24,512]{2,1,0:T(8,128)(2,1)}), bf16[64,24,512]{2,1,0:T(8,128)(2,1)S(1)}, u32[]{:S(2)}, u32[]{:S(2)}) async-start(bf16[64,24,512]{2,1,0:T(8,128)(2,1)} %broadcast_select_fusion), calls=%async_computation | async-start | bytes 3145728 | tf_op jit(solution)/shard_map/all_to_all | solution.py:65
  41.5 19.6 %copy-start.2 = (f32[128,512]{1,0:T(8,128)S(1)}, f32[128,512]{1,0:T(8,128)}, u32[]{:S(2)}) copy-start(f32[128,512]{1,0:T(8,128)} %param.11) | copy-start | bytes 786436
  41.5 86.5 %all-gather.2.cloned.1.call-start = ((), (), s32[]{:S(2)}) async-start(), calls=%async_computation.6 | async-start | bytes 2228224 | tf_op jit(solution)/shard_map/all_gather | solution.py:86
  87.6 3.4 copy-start.5
  87.6 3.4 copy-start.6
  90.1 112.2 %reduce-scatter.7.cloned.1.call-start = ((), (), s32[]{:S(2)}) async-start(), calls=%async_computation.7 | async-start | bytes 4456448 | tf_op jit(solution)/shard_map/reduce_scatter | solution.py:100
  202.3 2.4 copy-start.7
  204.7 7.1 %copy-start.8 = (f32[128,512]{1,0:T(8,128)}, f32[128,512]{1,0:T(8,128)S(1)}, u32[]{:S(2)}) copy-start(f32[128,512]{1,0:T(8,128)S(1)} %get-tuple-element.10) | copy-start | bytes 786436
  211.9 14.8 %copy-start.1 = (bf16[128,512]{1,0:T(8,128)(2,1)S(1)}, bf16[128,512]{1,0:T(8,128)(2,1)}, u32[]{:S(2)}) copy-start(bf16[128,512]{1,0:T(8,128)(2,1)} %multiply_convert_fusion.6) | copy-start | bytes 393220
  211.9 55.3 %all-to-all-start.1 = ((bf16[64,24,512]{2,1,0:T(8,128)(2,1)}), bf16[64,24,512]{2,1,0:T(8,128)(2,1)S(1)}, u32[]{:S(2)}, u32[]{:S(2)}) async-start(bf16[64,24,512]{2,1,0:T(8,128)(2,1)} %bitcast.51), calls=%async_computation.2 | async-start | bytes 3145728 | tf_op jit(solution)/shard_map/all_to_all | solution.py:122
  226.3 64.2 %reduce-scatter.13.cloned.1.call-start = ((), (), s32[]{:S(2)}) async-start(), calls=%async_computation.10 | async-start | bytes 139264
  227.8 128.3 %reduce-scatter.11.cloned.1.call-start = ((), (), s32[]{:S(2)}) async-start(), calls=%async_computation.9 | async-start | bytes 1114112 | tf_op jit(solution)/shard_map/reduce_scatter | solution.py:140
  230.3 190.1 %reduce-scatter.9.cloned.1.call-start = ((), (), s32[]{:S(2)}) async-start(), calls=%async_computation.8 | async-start | bytes 557056 | tf_op jit(solution)/shard_map/reduce_scatter | solution.py:137
Sparse Core Ops, SparseCore 0:
  90.3 37.7 all-gather.1
  135.0 67.2 reduce-scatter.6
  231.1 59.4 reduce-scatter.12
  294.2 61.8 reduce-scatter.10
  359.3 61.1 reduce-scatter.8
where the time goes:
time: 710 us
  waiting for transfers between devices  298 us (42%)
  blocking collectives  283 us (40%)
  other arithmetic  41.3 us (6%)
  starting transfers between devices  38.2 us (5%)
  matrix products  21.6 us (3%)
  between operations  14.1 us (2%)
  local copies, waits for them, and re-layouts  13.6 us (2%)
    psum x1, blocking collectives, body(): lax.psum((shares[0], shares[1], shares[2]), 'node')  283 us
    reduce_scatter x1, waiting for transfers between devices, body(): lax.psum_scatter(contract_rows(grad_bf, own_query), 'grp', scatter_dimens...  67.2 us
    reduce_scatter x1, waiting for transfers between devices, body(): lax.psum_scatter(comb_part.astype(jnp.bfloat16), 'grp', scatter_dimension...  64.7 us
    reduce_scatter x1, waiting for transfers between devices, body(): lax.psum_scatter(msg_part.astype(jnp.bfloat16), 'grp', scatter_dimension=...  64.4 us
    all_to_all x1, waiting for transfers between devices, body(): lax.all_to_all(returning.reshape(node_count, capacity, feat_width), 'node...  36.8 us
    all_gather x1, waiting for transfers between devices, body(): group_embed = lax.all_gather(embed, 'grp', axis=0, tiled=True)  33.7 us
    all_to_all x1, starting transfers between devices, body(): lax.all_to_all(outgoing, 'node', split_axis=0, concat_axis=0, tiled=True)  23.5 us
    all_to_all x1, waiting for transfers between devices, body(): lax.all_to_all(outgoing, 'node', split_axis=0, concat_axis=0, tiled=True)  21.5 us
  transfers between devices with their start and end apart: 7, of which 7 were waited for; matrix products, arithmetic and copies ran while one was open for 6% of the time, Pallas kernels for 0%

commit v1 on v0

v1 whole, which is shorter than its diff:
```python
import functools

import jax
import jax.numpy as jnp
from jax import lax
from jax.experimental import pallas as pl
from jax.experimental.pallas import tpu as pltpu
from jax.sharding import PartitionSpec as P

MESH = pl.DeviceIdType.MESH
F32, BF16, I32 = jnp.float32, jnp.bfloat16, jnp.int32
eps = 1e-05
LANES = 128
SPAN = 16
ROW = 8
FRONT = 16


def dot(left, right):
    return jnp.dot(left, right, preferred_element_type=F32)


def dot_nt(left, right):
    return lax.dot_general(left, right, (((1,), (1,)), ((), ())), preferred_element_type=F32)


def dot_tn(left, right):
    return lax.dot_general(left, right, (((0,), (0,)), ((), ())), preferred_element_type=F32)


def iota(shape, dim):
    return lax.broadcasted_iota(I32, shape, dim)


def ones_where(mask):
    return jnp.where(mask, 1.0, 0.0).astype(BF16)


def sigmoid(value):
    return 1.0 / (1.0 + jnp.exp(-value))


def silu_slope(value):
    logistic = sigmoid(value)
    return logistic * (1.0 + value * (1.0 - logistic))


def halves_stacked(value):
    mid = value.shape[1] // 2
    return jnp.concatenate([value[:, :mid], value[:, mid:]], axis=0)


def rows(start, size):
    return pl.ds(pl.multiple_of(start, size), size)


def as_column(row):
    return jnp.transpose(jnp.broadcast_to(row, (LANES, LANES)))


def greet(nodes, grps):
    node, grp = lax.axis_index("node"), lax.axis_index("grp")
    barrier = pltpu.get_barrier_semaphore()

    def hello_node(step, _):
        peer = (lax.rem(node + step, nodes), grp)
        pl.semaphore_signal(barrier, inc=1, device_id=peer, device_id_type=MESH)
        return 0

    def hello_grp(step, _):
        peer = (node, lax.rem(grp + step, grps))
        pl.semaphore_signal(barrier, inc=1, device_id=peer, device_id_type=MESH)
        return 0

    lax.fori_loop(1, nodes, hello_node, 0)
    lax.fori_loop(1, grps, hello_grp, 0)
    return lambda: pl.semaphore_wait(barrier, nodes + grps - 2)


class Exchange:
    def __init__(self, nodes, out_ref, in_ref, send_sem, recv_sem):
        self.nodes, self.planes = nodes, nodes // ROW
        self.out_ref, self.in_ref, self.send_sem, self.recv_sem = out_ref, in_ref, send_sem, recv_sem

    def peer(self, index, sign):
        me = lax.axis_index("node")
        dz = index % self.planes
        dy = (dz + index // self.planes) % ROW
        z = (me // ROW + self.planes + sign * dz) % self.planes
        return z * ROW + (me % ROW + ROW + sign * dy) % ROW

    def copy(self, index):
        at = rows(index * SPAN, SPAN)
        return pltpu.make_async_remote_copy(
            src_ref=self.out_ref.at[at, :],
            dst_ref=self.in_ref.at[at, :],
            send_sem=self.send_sem.at[index],
            recv_sem=self.recv_sem.at[index],
            device_id=(self.peer(index, 1), lax.axis_index("grp")),
            device_id_type=MESH,
        )

    def keep(self):
        self.in_ref[:SPAN, :] = self.out_ref[:SPAN, :]

    def start(self, first, last):
        lax.fori_loop(first, last, lambda i, _: (self.copy(i).start(), 0)[1], 0)

    def arrive(self, first, last):
        lax.fori_loop(first, last, lambda i, _: (self.copy(i).wait_recv(), 0)[1], 0)

    def finish(self):
        lax.fori_loop(1, self.nodes, lambda i, _: (self.copy(i).wait_send(), 0)[1], 0)


class Stage:
    def __init__(self, count, me, peer, source, landing, size, send_sem, recv_sem):
        self.count, self.me, self.peer, self.source = count, me, peer, source
        self.landing, self.size, self.send_sem, self.recv_sem = landing, size, send_sem, recv_sem

    def copy(self, to, place):
        return pltpu.make_async_remote_copy(
            src_ref=self.source(to),
            dst_ref=self.landing.at[rows(place * self.size, self.size), :],
            send_sem=self.send_sem.at[to],
            recv_sem=self.recv_sem.at[place],
            device_id=self.peer(to),
            device_id_type=MESH,
        )

    def each(self, act):
        def step(i, _):
            act(lax.rem(self.me + i, self.count))
            return 0

        lax.fori_loop(1, self.count, step, 0)

    def start(self):
        self.each(lambda to: self.copy(to, self.me).start())

    def arrive(self):
        self.each(lambda source: self.copy(source, source).wait_recv())

    def finish(self):
        self.each(lambda to: self.copy(to, self.me).wait_send())

    def total(self, own):
        def add(i, acc):
            source = lax.rem(self.me + i, self.count)
            return acc + self.landing[rows(source * self.size, self.size), :].astype(F32)

        return lax.fori_loop(1, self.count, add, own)


def to_pieces(value, ref):
    per = ref.shape[1] // LANES
    wide = value.shape[1] // LANES
    for k in range(value.shape[0] // 8 * wide):
        r, c = divmod(k, wide)
        piece, place = divmod(k, per)
        ref[piece * 8 : piece * 8 + 8, place * LANES : place * LANES + LANES] = value[
            r * 8 : r * 8 + 8, c * LANES : c * LANES + LANES
        ]


def from_pieces(ref, shape):
    per = ref.shape[1] // LANES
    wide = shape[1] // LANES
    bands = []
    for r in range(shape[0] // 8):
        band = []
        for c in range(wide):
            piece, place = divmod(r * wide + c, per)
            band.append(ref[piece * 8 : piece * 8 + 8, place * LANES : place * LANES + LANES])
        bands.append(jnp.concatenate(band, axis=1))
    return jnp.concatenate(bands, axis=0)


class NodeSum:
    def __init__(self, nodes, pieces, z_in, mine, y_in, full, sems):
        node, grp = lax.axis_index("node"), lax.axis_index("grp")
        planes = nodes // ROW
        self.z, self.y = node // ROW, lax.rem(node, ROW)
        z, y = self.z, self.y
        self.pieces, self.mine, self.y_in, self.full = pieces, mine, y_in, full

        def z_peer(to):
            return (to * ROW + y, grp)

        def y_peer(to):
            return (z * ROW + to, grp)

        self.first = Stage(planes, z, z_peer, lambda to: pieces.at[rows(to * 8, 8), :], z_in, 8, sems[0], sems[1])
        self.second = Stage(ROW, y, y_peer, lambda to: mine, y_in, 8, sems[2], sems[3])
        self.third = Stage(planes, z, z_peer, lambda to: full.at[rows(z * 8, 8), :], full, 8, sems[4], sems[5])

    def begin(self, value):
        if self.pieces.shape[0] * self.pieces.shape[1] > value.shape[0] * value.shape[1]:
            self.pieces[...] = jnp.zeros_like(self.pieces)
        to_pieces(value, self.pieces)
        self.first.start()

    def over_y(self):
        self.first.arrive()
        own = self.first.total(self.pieces[rows(self.z * 8, 8), :])
        self.mine[...] = own
        self.y_in[rows(self.y * 8, 8), :] = own
        self.second.start()

    def gather(self):
        self.second.arrive()
        total = self.y_in[:8, :]
        for k in range(1, ROW):
            total = total + self.y_in[k * 8 : k * 8 + 8, :]
        self.full[rows(self.z * 8, 8), :] = total
        self.third.start()

    def end(self):
        self.third.arrive()

    def finish(self):
        for stage in (self.first, self.second, self.third):
            stage.finish()


class Ring:
    def __init__(self, grps, all_ref, size, send_sem, recv_sem):
        node, me = lax.axis_index("node"), lax.axis_index("grp")
        self.node, self.me, self.all_ref, self.size = node, me, all_ref, size
        self.send_sem, self.recv_sem = send_sem, recv_sem
        self.chips, self.core, self.chip = grps // 2, lax.rem(me, 2), me // 2
        self.hops = self.chips // 2
        self.index, self.started = {}, []
        for side in (0, 1):
            for hop in range(1, self.hops + 1):
                for piece in (0, 1):
                    if hop < self.hops or piece == side:
                        self.index["link", side, hop, piece] = len(self.index)
        for key in list(self.index):
            self.index[("core",) + key[1:]] = len(self.index)
        for piece in (0, 1):
            self.index["core", 0, 0, piece] = len(self.index)

    def at_chip(self, steps):
        return lax.rem(self.chip + self.chips + steps, self.chips) * 2 + self.core

    def origin(self, side, hop):
        return self.at_chip(-hop if side == 0 else hop)

    def copy(self, key):
        kind, side, hop, piece = key
        origin = self.origin(side, hop - 1 if kind == "link" else hop)
        half = self.size // 2
        at = rows(origin * self.size + piece * half, half)
        to = self.at_chip(1 if side == 0 else -1) if kind == "link" else self.chip * 2 + 1 - self.core
        return pltpu.make_async_remote_copy(
            src_ref=self.all_ref.at[at, :],
            dst_ref=self.all_ref.at[at, :],
            send_sem=self.send_sem.at[self.index[key]],
            recv_sem=self.recv_sem.at[self.index[key]],
            device_id=(self.node, to),
            device_id_type=MESH,
        )

    def start(self, *key):
        if key in self.index:
            self.copy(key).start()
            self.started.append(key)

    def arrive(self, *key):
        if key in self.index:
            self.copy(key).wait_recv()

    def begin(self):
        for piece in (0, 1):
            for side in (0, 1):
                self.start("link", side, 1, piece ^ side)
        for piece in (0, 1):
            self.start("core", 0, 0, piece)

    def step(self, hop):
        for piece in (0, 1):
            for side in (0, 1):
                key = (side, hop, piece ^ side)
                self.arrive("link", *key)
                self.start("link", side, hop + 1, piece ^ side)
                if ("link", *key) in self.index:
                    self.start("core", *key)

    def other(self, hop):
        for side in (0, 1):
            for piece in (0, 1):
                if hop or side == 0:
                    self.arrive("core", side, hop, piece)

    def finish(self):
        for key in self.started:
            self.copy(key).wait_send()


def tower_kernel(
    nodes, grps, nbr_ref, tgt_ref, msgw_ref, combw_ref, gain_ref, served_ref, owners_ref, weight_ref, labels_ref, pos_ref,
    loss_ref, gmsg_ref, gcomb_ref, ghead_ref,
    msg_ref, msg2_ref, bf_ref, slope_ref, serve_ref,
    out_ref, in_ref, send_sem, recv_sem, a1_ref, a2_ref, at1_ref, at2_ref, front_ref, back_ref, comb_in_ref, pre_ref,
    all_ref, query_ref, gains_ref, rt_ref, ct_ref, ring_send, ring_recv, stat_ref, stat_send, stat_recv,
    out2_ref, in2_ref, send2_sem, recv2_sem, acc_ref, acc2_ref,
    cpart_ref, cland_ref, cpart_send, cpart_recv, cpieces, cz_in, cmine, cy_in, cfull, c0, c1, c2, c3, c4, c5,
    mpart_ref, pair_ref, pair_send, pair_recv, mhalf_ref, mland_ref, mx_send, mx_recv,
    mpieces, mz_in, mmine, my_in, mfull, m0, m1, m2, m3, m4, m5,
):
    ready = greet(nodes, grps)
    node, me = lax.axis_index("node"), lax.axis_index("grp")
    feat, tgts, pins = msgw_ref.shape[0], tgt_ref.shape[0], nbr_ref.shape[0]
    half, planes, span, group = feat // 2, nodes // ROW, nodes * SPAN, tgts * grps
    chunks = span // LANES
    per = LANES // SPAN
    lane = iota((LANES, LANES), 1)
    sub = iota((LANES, LANES), 0)

    def message(tile, _):
        at = rows(tile * LANES, LANES)
        nbr = nbr_ref[at, :].astype(BF16)
        bf_ref[at, :] = nbr
        pre = dot(nbr, msgw_ref[...])
        slope_ref[at, :] = pre
        msg = (pre * sigmoid(pre)).astype(BF16)
        msg_ref[at, :] = msg
        msg2_ref[at, :] = msg[:, :half]
        msg2_ref[rows(pins + tile * LANES, LANES), :] = msg[:, half:]
        return 0

    lax.fori_loop(0, pins // LANES, message, 0)
    serve_ref[...] = jnp.zeros_like(serve_ref)
    serve_ref[: served_ref.shape[0], : served_ref.shape[1]] = served_ref[...]
    forth = Exchange(nodes, out_ref, in_ref, send_sem, recv_sem)
    back = Exchange(nodes, out2_ref, in2_ref, send2_sem, recv2_sem)

    def keys_of(chunk, sign):
        peers = forth.peer(sub // SPAN + chunk * per, sign)
        pick = ones_where(lane == peers)
        table = serve_ref[...]
        upper = (table // 2).astype(F32).astype(BF16)
        lower = (table % 2).astype(F32).astype(BF16)
        listed = dot(pick, upper) * 2.0 + dot(pick, lower)
        place = sub % SPAN
        key1 = jnp.sum(jnp.where(lane == place, listed, 0.0), axis=1, keepdims=True)
        key2 = jnp.sum(jnp.where(lane == FRONT + place % 8, listed, 0.0), axis=1, keepdims=True)
        key1 = jnp.broadcast_to(key1, (LANES, LANES))
        key2 = jnp.broadcast_to(key2, (LANES, LANES)) + jnp.where(place >= 8, float(pins), 0.0)
        return key1.astype(I32), key2.astype(I32)

    ready()

    def serve(chunk, _):
        at = rows(chunk * LANES, LANES)
        key1, key2 = keys_of(chunk, 1)
        pick1 = jnp.concatenate([ones_where(key1 == lane + c * LANES) for c in range(pins // LANES)], 1)
        pick2 = jnp.concatenate([ones_where(key2 == lane + c * LANES) for c in range(2 * pins // LANES)], 1)
        out_ref[at, :feat] = dot(pick1, msg_ref[...]).astype(BF16)
        out_ref[at, feat:] = dot(pick2, msg2_ref[...]).astype(BF16)
        forth.start(jnp.maximum(chunk * per, 1), chunk * per + per)
        return 0

    lax.fori_loop(0, chunks, serve, 0)
    forth.keep()

    hits_t = jnp.zeros((LANES, tgts), F32)
    weights_t = jnp.zeros((LANES, tgts), F32)
    for k in range(owners_ref.shape[0]):
        hit = owners_ref[k : k + 1, :] == sub
        hits_t = hits_t + jnp.where(hit, 1.0, 0.0)
        weights_t = weights_t + jnp.where(hit, weight_ref[k : k + 1, :].astype(F32), 0.0)
    above = ones_where(sub < lane)
    earlier_t = dot(hits_t.astype(BF16), above)
    weights = jnp.transpose(weights_t)
    total = jnp.sum(weights, axis=1, keepdims=True)
    earlier = jnp.transpose(earlier_t).astype(BF16)
    weights, earlier_t, weights_t = weights.astype(BF16), earlier_t.astype(BF16), weights_t.astype(BF16)

    def weigh(chunk, _):
        at = rows(chunk * LANES, LANES)
        spread = ones_where(sub == forth.peer(lane // SPAN + chunk * per, -1))
        slot, weight = dot(earlier, spread), dot(weights, spread)
        place = lane % SPAN
        a1_ref[:, at] = jnp.where(slot == place.astype(F32), weight, 0.0).astype(BF16)
        late = jnp.where(slot == (FRONT + place % 8).astype(F32), weight, 0.0)
        a2_ref[:tgts, at] = jnp.where(place < 8, late, 0.0).astype(BF16)
        a2_ref[tgts:, at] = jnp.where(place >= 8, late, 0.0).astype(BF16)
        spread = ones_where(lane == forth.peer(sub // SPAN + chunk * per, 1))
        slot, weight = dot(spread, earlier_t), dot(spread, weights_t)
        place = sub % SPAN
        at1_ref[at, :] = jnp.where(slot == place.astype(F32), weight, 0.0).astype(BF16)
        late = jnp.where(slot == (FRONT + place % 8).astype(F32), weight, 0.0)
        at2_ref[at, :tgts] = jnp.where(place < 8, late, 0.0).astype(BF16)
        at2_ref[at, tgts:] = jnp.where(place >= 8, late, 0.0).astype(BF16)
        return 0

    lax.fori_loop(0, chunks, weigh, 0)

    tgt_bf = tgt_ref[...].astype(BF16)
    comb_in_ref[:, :feat] = tgt_bf
    pre_ref[...] = dot(tgt_bf, combw_ref[:feat, :])

    def slopes(tile, _):
        at = rows(tile * LANES, LANES)
        slope_ref[at, :] = silu_slope(slope_ref[at, :])
        return 0

    lax.fori_loop(0, pins // LANES, slopes, 0)
    gain = gain_ref[...]
    gain_hi = gain.astype(BF16).astype(F32)
    gain_mid = (gain - gain_hi).astype(BF16).astype(F32)
    gain_lo = gain - gain_hi - gain_mid
    tasks = gain.shape[0]
    gain3 = jnp.concatenate(
        [gain_hi, gain_mid, gain_lo, jnp.zeros((LANES - 3 * tasks, feat), F32)], axis=0
    ).astype(BF16)

    def gains(block, _):
        label = as_column(labels_ref[pl.ds(block, 1), :])
        pick = ones_where((label == lane % tasks) & (lane < 3 * tasks))
        gains_ref[rows(block * tgts, tgts), :] = dot(pick, gain3)
        return 0

    lax.fori_loop(0, grps, gains, 0)
    front_ref[...] = jnp.zeros_like(front_ref)
    back_ref[...] = jnp.zeros_like(back_ref)
    acc_ref[...] = jnp.zeros_like(acc_ref)
    acc2_ref[...] = jnp.zeros_like(acc2_ref)

    def collect(chunk, _):
        at = rows(chunk * LANES, LANES)
        forth.arrive(jnp.maximum(chunk * per, 1), chunk * per + per)
        front_ref[...] += dot(a1_ref[:, at], in_ref[at, :feat])
        back_ref[...] += dot(a2_ref[:, at], in_ref[at, feat:])
        return 0

    lax.fori_loop(0, chunks, collect, 0)
    aggregate = front_ref[...] + jnp.concatenate([back_ref[:tgts, :], back_ref[tgts:, :]], axis=1)
    agg_bf = (aggregate / total).astype(BF16)
    comb_in_ref[:, feat:] = agg_bf
    comb_pre = pre_ref[...] + dot(agg_bf, combw_ref[feat:, :])
    pre_ref[...] = comb_pre
    hidden = comb_pre * sigmoid(comb_pre)
    inv_norm = lax.rsqrt(jnp.mean(hidden * hidden, axis=1, keepdims=True) + eps)
    embed = (hidden * inv_norm).astype(BF16)

    own = rows(me * tgts, tgts)
    all_ref[own, :] = embed
    ring = Ring(grps, all_ref, tgts, ring_send, ring_recv)
    ring.begin()
    own_gain = gains_ref[own, :]
    own_query = (embed.astype(F32) * own_gain).astype(BF16)

    def score(block):
        at = rows(block * tgts, tgts)
        block_embed = all_ref[at, :]
        block_query = (block_embed.astype(F32) * gains_ref[at, :]).astype(BF16)
        query_ref[at, :] = block_query
        rt_ref[at, :] = dot_nt(block_embed, own_query) / feat
        ct_ref[at, :] = dot_nt(all_ref[own, :], block_query) / feat

    score(me)
    for hop in range(1, ring.hops + 1):
        ring.step(hop)
        ring.other(hop - 1)
        if hop < ring.hops:
            score(ring.origin(0, hop))
            score(ring.origin(1, hop))
        else:
            score(ring.origin(0, hop))
        for side in (0, 1) if hop > 1 else (0,):
            score(ring.origin(side, hop - 1) + 1 - 2 * ring.core)
    ring.other(ring.hops)
    score(ring.origin(0, ring.hops) + 1 - 2 * ring.core)

    scores = rt_ref[...]
    top = jnp.max(scores, axis=0, keepdims=True)
    terms = jnp.exp(scores - top)
    norm = jnp.sum(terms, axis=0, keepdims=True)
    own_stat = rows(me * 8, 8)
    stat_ref[own_stat, :] = jnp.concatenate(
        [jnp.broadcast_to(top, (4, LANES)), jnp.broadcast_to(norm, (4, LANES))], axis=0
    )
    stats = Stage(grps, me, lambda to: (node, to), lambda to: stat_ref.at[own_stat, :], stat_ref, 8, stat_send, stat_recv)
    stats.start()
    hit = jnp.where(iota((group, tgts), 0) == pos_ref[pl.ds(me, 1), :], 1.0, 0.0)
    picked = jnp.sum(scores * hit, axis=0, keepdims=True)
    loss_ref[...] = top + jnp.log(norm) - picked
    grad = ((terms / norm - hit) / group / feat).astype(BF16)
    query_grad = dot_tn(grad, all_ref[...])
    stats.arrive()

    def column(block, acc):
        at = rows(block * tgts, tgts)
        stat = stat_ref[rows(block * 8, 8), :]
        terms = jnp.exp(ct_ref[at, :] - stat[0:1, :]) / stat[4:5, :]
        mine = iota((tgts, LANES), 0) + me * tgts == pos_ref[pl.ds(block, 1), :]
        grad = ((terms - jnp.where(mine, 1.0, 0.0)) / group / feat).astype(BF16)
        return acc + dot(grad, query_ref[at, :])

    column_grad = lax.fori_loop(0, grps, column, jnp.zeros((tgts, feat), F32))
    embed_grad = query_grad * own_gain + column_grad
    logistic = sigmoid(comb_pre)
    inner = jnp.sum(hidden * embed_grad, axis=1, keepdims=True)
    cube = inv_norm * inv_norm * inv_norm
    hidden_grad = inv_norm * embed_grad - hidden * (cube * inner / feat)
    slope = logistic * (1.0 + comb_pre * (1.0 - logistic))
    pre_grad = (slope * hidden_grad).astype(BF16)
    agg = dot_nt(pre_grad, combw_ref[feat:, :]) / total

    agg_hi = agg.astype(BF16)
    agg_lo = (agg - agg_hi.astype(F32)).astype(BF16)
    both = jnp.concatenate([agg_hi, agg_lo], axis=0)
    both2 = jnp.concatenate([halves_stacked(agg_hi), halves_stacked(agg_lo)], axis=0)

    def give(chunk, _):
        at = rows(chunk * LANES, LANES)
        w1, w2 = at1_ref[at, :], at2_ref[at, :]
        out2_ref[at, :feat] = dot(jnp.concatenate([w1, w1], axis=1), both).astype(BF16)
        out2_ref[at, feat:] = dot(jnp.concatenate([w2, w2], axis=1), both2).astype(BF16)
        back.start(jnp.maximum(chunk * per, 1), chunk * per + per)
        return 0

    lax.fori_loop(0, chunks, give, 0)
    back.keep()

    cols = feat // grps
    cpart_ref[:, : 2 * feat] = dot_tn(pre_grad, comb_in_ref[...]).astype(BF16)
    pick = ones_where(as_column(labels_ref[pl.ds(me, 1), :]) == lane)
    head = query_grad * embed.astype(F32)
    head_hi = head.astype(BF16)
    head_lo = (head - head_hi.astype(F32)).astype(BF16)
    cpart_ref[:, 2 * feat :] = (dot_tn(head_hi, pick) + dot_tn(head_lo, pick)).astype(BF16)
    comb_sum = Stage(
        grps, me, lambda to: (node, to), lambda to: cpart_ref.at[rows(to * cols, cols), :], cland_ref, cols, cpart_send, cpart_recv
    )
    comb_sum.start()
    comb_full = NodeSum(nodes, cpieces, cz_in, cmine, cy_in, cfull, (c0, c1, c2, c3, c4, c5))
    msg_full = NodeSum(nodes, mpieces, mz_in, mmine, my_in, mfull, (m0, m1, m2, m3, m4, m5))

    def take(chunk, _):
        at = rows(chunk * LANES, LANES)
        key1, key2 = keys_of(chunk, -1)
        key1, key2 = jnp.transpose(key1), jnp.transpose(key2)
        spread1 = jnp.concatenate([ones_where(key1 == sub + c * LANES) for c in range(pins // LANES)], 0)
        spread2 = jnp.concatenate([ones_where(key2 == sub + c * LANES) for c in range(2 * pins // LANES)], 0)
        back.arrive(jnp.maximum(chunk * per, 1), chunk * per + per)
        acc_ref[...] += dot(spread1, in2_ref[at, :feat])
        acc2_ref[...] += dot(spread2, in2_ref[at, feat:])
        return 0

    lax.fori_loop(0, chunks - 2, take, 0)
    comb_sum.arrive()
    comb_full.begin(comb_sum.total(cpart_ref[rows(me * cols, cols), :].astype(F32)))
    lax.fori_loop(chunks - 2, chunks, take, 0)

    row_grad = acc_ref[...] + jnp.concatenate([acc2_ref[:pins, :], acc2_ref[pins:, :]], axis=1)
    msg_grad = (slope_ref[...] * row_grad).astype(BF16)
    part = dot_tn(msg_grad, bf_ref[...]).astype(BF16)
    for g in range(grps):
        first = (g % 2) * half + (g // 2) * cols
        mpart_ref[first : first + cols, :] = part[g * cols : g * cols + cols, :]
    core, chip = lax.rem(me, 2), me // 2
    pair = pltpu.make_async_remote_copy(
        src_ref=mpart_ref.at[rows((1 - core) * half, half), :],
        dst_ref=pair_ref,
        send_sem=pair_send,
        recv_sem=pair_recv,
        device_id=(node, chip * 2 + 1 - core),
        device_id_type=MESH,
    )
    pair.start()
    comb_full.over_y()
    pair.wait_recv()
    mhalf_ref[...] = (mpart_ref[rows(core * half, half), :].astype(F32) + pair_ref[...].astype(F32)).astype(BF16)
    over_x = Stage(
        grps // 2, chip, lambda to: (node, to * 2 + core), lambda to: mhalf_ref.at[rows(to * cols, cols), :], mland_ref, cols, mx_send, mx_recv
    )
    over_x.start()
    comb_full.gather()
    over_x.arrive()
    msg_full.begin(over_x.total(mhalf_ref[rows(chip * cols, cols), :].astype(F32)))
    comb_full.end()
    comb_value = from_pieces(cfull, (cols, 2 * feat + LANES))
    gcomb_ref[...] = comb_value[:, : 2 * feat]
    head_value = comb_value[:, 2 * feat :]
    if cols < LANES:
        head_value = jnp.concatenate([head_value, jnp.zeros((LANES - cols, LANES), F32)], axis=0)
    ghead_ref[...] = jnp.transpose(head_value)[:tasks, :]
    msg_full.over_y()
    msg_full.gather()
    forth.finish()
    ring.finish()
    stats.finish()
    back.finish()
    comb_sum.finish()
    comb_full.finish()
    pair.wait_send()
    over_x.finish()
    msg_full.end()
    gmsg_ref[...] = from_pieces(mfull, (cols, feat))
    msg_full.finish()


def body(
    nodes, grps, nbr_feats, tgt_feats, msg_weight, comb_weight, head_gain, owners, serve_rows, importance,
    labels, positives,
):
    pins, feat = nbr_feats.shape
    tgts, tasks = tgt_feats.shape[0], head_gain.shape[0]
    group, span, half = tgts * grps, nodes * SPAN, feat // 2
    cols, planes, chips = feat // grps, nodes // ROW, grps // 2
    hops = chips // 2
    links = 2 * max(2 * hops - 1, 0)
    block = feat + half
    wide = 2 * feat + LANES

    def vm(kind, *shape):
        return pltpu.VMEM(shape, kind)

    def dma(*shape):
        return pltpu.SemaphoreType.DMA(shape)

    def sum_scratch(width):
        per = -(-(cols // 8 * (width // LANES)) // planes) * LANES
        piece = [vm(F32, planes * 8, per), vm(F32, planes * 8, per), vm(F32, 8, per), vm(F32, ROW * 8, per), vm(F32, planes * 8, per)]
        return piece + [dma(planes), dma(planes), dma(ROW), dma(ROW), dma(planes), dma(planes)]

    scratch = [
        vm(BF16, pins, feat), vm(BF16, 2 * pins, half), vm(BF16, pins, feat), vm(F32, pins, feat), vm(I32, LANES, LANES),
        vm(BF16, span, block), vm(BF16, span, block), dma(nodes), dma(nodes),
        vm(BF16, tgts, span), vm(BF16, 2 * tgts, span), vm(BF16, span, tgts), vm(BF16, span, 2 * tgts),
        vm(F32, tgts, feat), vm(F32, 2 * tgts, half), vm(BF16, tgts, 2 * feat), vm(F32, tgts, feat),
        vm(BF16, group, feat), vm(BF16, group, feat), vm(F32, group, feat), vm(F32, group, tgts), vm(F32, group, tgts),
        dma(2 * links + 2), dma(2 * links + 2), vm(F32, grps * 8, LANES), dma(grps), dma(grps),
        vm(BF16, span, block), vm(BF16, span, block), dma(nodes), dma(nodes), vm(F32, pins, feat), vm(F32, 2 * pins, half),
        vm(BF16, feat, wide), vm(BF16, feat, wide), dma(grps), dma(grps), *sum_scratch(wide),
        vm(BF16, feat, feat), vm(BF16, half, feat), pltpu.SemaphoreType.DMA, pltpu.SemaphoreType.DMA,
        vm(BF16, half, feat), vm(BF16, half, feat), dma(chips), dma(chips), *sum_scratch(feat),
    ]
    args = (
        nbr_feats, tgt_feats, msg_weight, comb_weight, head_gain, serve_rows[0], owners.T, importance.T,
        labels.reshape(grps, tgts), positives.reshape(grps, tgts),
    )
    whole = pl.BlockSpec(memory_space=pltpu.VMEM)
    outs = [(1, tgts), (cols, feat), (cols, 2 * feat), (tasks, max(cols, LANES))]
    loss, grad_msg, grad_comb, grad_head = pl.pallas_call(
        functools.partial(tower_kernel, nodes, grps),
        name="tower",
        out_shape=[jax.ShapeDtypeStruct(shape, F32) for shape in outs],
        in_specs=[whole] * len(args),
        out_specs=[whole] * len(outs),
        scratch_shapes=scratch,
        compiler_params=pltpu.CompilerParams(
            collective_id=0, has_side_effects=True, vmem_limit_bytes=60 * 2**20
        ),
    )(*args)
    return loss.reshape(tgts), grad_msg.T, grad_comb.T, grad_head[:, :cols]


def solution(mesh):
    placed = (
        P(("node", "grp"), None),
        P(("node", "grp"), None),
        P(),
        P(),
        P(),
        P(("node", "grp"), None),
        P(("node", "grp"), None, None),
        P(("node", "grp"), None),
        P("node"),
        P("node"),
    )
    return jax.shard_map(
        functools.partial(body, mesh.shape["node"], mesh.shape["grp"]),
        mesh=mesh,
        in_specs=placed,
        out_specs=(P(("node", "grp")), P(None, "grp"), P(None, "grp"), P(None, "grp")),
        check_vma=False,
    )
```

time: 710 us -> 172 us (0.24)
  the two profiles are of different devices: /device:TPU:8 before, /device:TPU:4 now
where the time goes in v1:
time: 172 us
  Pallas kernels  166 us (97%)
  local copies, waits for them, and re-layouts  5.36 us (3%)
    pallas_call x1, Pallas kernels, body(): pl.pallas_call(functools.partial(tower_kernel, nodes, grps), name='tower'...  166 us
    unnamed x9, local copies, waits for them, and re-layouts  5.36 us

profile of v1, /device:TPU:4, one launch (start us, length us, event | category | flops | bytes accessed | tf_op | source)
XLA Modules:
  0.0 171.9 jit_solution(1536795359367342361)
XLA Ops:
  0.6 1.4 copy.14
  2.0 165.8 %tower.1 = (f32[1,128]{1,0:T(1,128)}, f32[32,512]{1,0:T(8,128)}, f32[32,1024]{1,0:T(8,128)}, f32[8,128]{1,0:T(8,128)}) custom-call(f32[512,512]{1,0:T(8,128)} %nbr_ref.1, f32[128,512]{1,0:T(8,128)} %tgt_ref.1, bf16[512,512]{1,0:T(8,128)(2,1)} %msgw_ref.1, bf16[1024,512]{1,0:T(8,128)(2,1)} %combw_ref.1, f32[8,512]{1,0:T(8,128)} %gain_ref.1, ...), custom_call_target="tpu_custom_call" | custom-call | tf_op jit(solution)/shard_map/tower/pallas_call | solution.py:649
  167.9 0.0 copy-start
  167.9 1.2 copy.19
  169.1 1.5 copy.20
  170.6 0.0 copy-done
  170.6 0.0 copy-start.1
  170.6 0.7 copy.21
  171.2 0.0 copy-done.1
  171.3 0.6 copy.22
Async XLA Ops:
  167.9 2.7 %copy-start = (f32[32,1024]{1,0:T(8,128)S(1)}, f32[32,1024]{1,0:T(8,128)}, u32[]{:S(2)}) copy-start(f32[32,1024]{1,0:T(8,128)} %get-tuple-element.10) | copy-start | bytes 393220
  170.6 0.7 copy-start.1

commit v2 on v1

--- a/solution.py
+++ b/solution.py
@@ -11,9 +11,7 @@
 F32, BF16, I32 = jnp.float32, jnp.bfloat16, jnp.int32
 eps = 1e-05
 LANES = 128
-SPAN = 16
 ROW = 8
-FRONT = 16
 
 
 def dot(left, right):
@@ -43,11 +41,6 @@
 def silu_slope(value):
     logistic = sigmoid(value)
     return logistic * (1.0 + value * (1.0 - logistic))
-
-
-def halves_stacked(value):
-    mid = value.shape[1] // 2
-    return jnp.concatenate([value[:, :mid], value[:, mid:]], axis=0)
 
 
 def rows(start, size):
@@ -77,40 +70,8 @@
     return lambda: pl.semaphore_wait(barrier, nodes + grps - 2)
 
 
-class Exchange:
-    def __init__(self, nodes, out_ref, in_ref, send_sem, recv_sem):
-        self.nodes, self.planes = nodes, nodes // ROW
-        self.out_ref, self.in_ref, self.send_sem, self.recv_sem = out_ref, in_ref, send_sem, recv_sem
-
-    def peer(self, index, sign):
-        me = lax.axis_index("node")
-        dz = index % self.planes
-        dy = (dz + index // self.planes) % ROW
-        z = (me // ROW + self.planes + sign * dz) % self.planes
-        return z * ROW + (me % ROW + ROW + sign * dy) % ROW
-
-    def copy(self, index):
-        at = rows(index * SPAN, SPAN)
-        return pltpu.make_async_remote_copy(
-            src_ref=self.out_ref.at[at, :],
-            dst_ref=self.in_ref.at[at, :],
-            send_sem=self.send_sem.at[index],
-            recv_sem=self.recv_sem.at[index],
-            device_id=(self.peer(index, 1), lax.axis_index("grp")),
-            device_id_type=MESH,
-        )
-
-    def keep(self):
-        self.in_ref[:SPAN, :] = self.out_ref[:SPAN, :]
-
-    def start(self, first, last):
-        lax.fori_loop(first, last, lambda i, _: (self.copy(i).start(), 0)[1], 0)
-
-    def arrive(self, first, last):
-        lax.fori_loop(first, last, lambda i, _: (self.copy(i).wait_recv(), 0)[1], 0)
-
-    def finish(self):
-        lax.fori_loop(1, self.nodes, lambda i, _: (self.copy(i).wait_send(), 0)[1], 0)
+def offset(step, count):
+    return lax.rem(jnp.where(lax.rem(step, 2) == 1, (step + 1) // 2, count - step // 2), count)
 
 
 class Stage:
@@ -130,7 +91,7 @@
 
     def each(self, act):
         def step(i, _):
-            act(lax.rem(self.me + i, self.count))
+            act(lax.rem(self.me + offset(i, self.count), self.count))
             return 0
 
         lax.fori_loop(1, self.count, step, 0)
@@ -174,6 +135,116 @@
             band.append(ref[piece * 8 : piece * 8 + 8, place * LANES : place * LANES + LANES])
         bands.append(jnp.concatenate(band, axis=1))
     return jnp.concatenate(bands, axis=0)
+
+
+class Path:
+    def __init__(self, nodes, y_first, cap, refs, sems):
+        node, self.grp = lax.axis_index("node"), lax.axis_index("grp")
+        planes = nodes // ROW
+        z, y = node // ROW, lax.rem(node, ROW)
+        self.y_first = y_first
+        self.firsts, self.seconds = (ROW, planes) if y_first else (planes, ROW)
+        self.me1, self.me2 = (y, z) if y_first else (z, y)
+        self.block = cap * self.seconds
+        (self.tab, self.ws, self.es, self.wt, self.et, self.a, self.at, self.pt, self.out, self.inn, self.sums, self.sent, self.land,
+         self.agg, self.out2, self.in2) = refs
+        block, me1, me2 = self.block, self.me1, self.me2
+        firsts, seconds, peer1, peer2 = self.firsts, self.seconds, self.peer1, self.peer2
+
+        def own_tab(to):
+            return self.tab.at[rows(me2 * 16, 16), :]
+
+        def own_agg(to):
+            return self.agg.at[rows(me2 * LANES, LANES), :]
+
+        self.tables = Stage(seconds, me2, peer2, own_tab, self.tab, 16, sems[0], sems[1])
+        self.rows_out = Stage(firsts, me1, peer1, lambda to: self.out.at[rows(to * block, block), :], self.inn, block, sems[2], sems[3])
+        self.sums_out = Stage(seconds, me2, peer2, lambda to: self.sent.at[rows(to * LANES, LANES), :], self.land, LANES, sems[4], sems[5])
+        self.agg_out = Stage(seconds, me2, peer2, own_agg, self.agg, LANES, sems[6], sems[7])
+        self.rows_back = Stage(firsts, me1, peer1, lambda to: self.out2.at[rows(to * block, block), :], self.in2, block, sems[8], sems[9])
+
+    def node_of(self, first, second):
+        return second * ROW + first if self.y_first else first * ROW + second
+
+    def peer1(self, to):
+        return (self.node_of(to, self.me2), self.grp)
+
+    def peer2(self, to):
+        return (self.node_of(self.me1, to), self.grp)
+
+    def first(self, step):
+        return lax.rem(self.me1 + offset(step, self.firsts), self.firsts)
+
+    def put_tables(self, owners, weights):
+        self.tab[rows(self.me2 * 16, 8), :] = owners
+        self.tab[rows(self.me2 * 16 + 8, 8), :] = weights
+
+    def key_column(self, first, upper, lower):
+        sub, lane = iota((self.block, LANES), 0), iota((self.block, LANES), 1)
+        pick = ones_where(lane == self.node_of(first, sub % self.seconds))
+        listed = dot_nt(pick, upper) * 2.0 + dot_nt(pick, lower)
+        return jnp.sum(jnp.where(lane == sub // self.seconds, listed, 0.0), axis=1, keepdims=True)
+
+    def key_row(self, first, upper, lower):
+        sub, lane = iota((self.block, LANES), 0), iota((self.block, LANES), 1)
+        pick = ones_where(lane == self.node_of(first, sub % self.seconds))
+        listed = dot_nt(upper, pick) * 2.0 + dot_nt(lower, pick)
+        sub, lane = iota((LANES, self.block), 0), iota((LANES, self.block), 1)
+        return jnp.sum(jnp.where(sub == lane // self.seconds, listed, 0.0), axis=0, keepdims=True)
+
+    def serve(self, first, upper, lower, messages):
+        key = self.key_column(first, upper, lower)
+        pick = ones_where(key == iota((self.block, messages.shape[0]), 1).astype(F32))
+        self.out[rows(first * self.block, self.block), :] = dot(pick, messages[...]).astype(BF16)
+
+    def keep(self, out, inn):
+        own = rows(self.me1 * self.block, self.block)
+        inn[own, :] = out[own, :]
+
+    def read_tables(self, above):
+        sub = iota((LANES, LANES), 0)
+
+        def read(second, _):
+            hits = jnp.zeros((LANES, LANES), F32)
+            weights = jnp.zeros((LANES, LANES), F32)
+            for k in range(8):
+                hit = self.tab[pl.ds(second * 16 + k, 1), :] == sub
+                hits = hits + jnp.where(hit, 1.0, 0.0)
+                weights = weights + jnp.where(hit, self.tab[pl.ds(second * 16 + 8 + k, 1), :].astype(F32), 0.0)
+            earlier = dot(hits.astype(BF16), above)
+            at = rows(second * LANES, LANES)
+            self.wt[:, at] = weights
+            self.et[:, at] = earlier
+            self.ws[at, :] = jnp.transpose(weights).astype(BF16)
+            self.es[at, :] = jnp.transpose(earlier).astype(BF16)
+            return 0
+
+        lax.fori_loop(0, self.seconds, read, 0)
+
+    def weigh(self, first):
+        tall = self.seconds * LANES
+        owner = self.node_of(first, self.me2)
+        spread = ones_where(iota((LANES, self.block), 0) == owner)
+        weight, slot = dot(self.ws[...], spread), dot(self.es[...], spread)
+        sub, lane = iota((tall, self.block), 0), iota((tall, self.block), 1)
+        mine = (lane % self.seconds == sub // LANES) & (slot == (lane // self.seconds).astype(F32))
+        self.a[first] = jnp.where(mine, weight, 0.0).astype(BF16)
+
+    def weigh_back(self, first):
+        tall = self.seconds * LANES
+        owner = self.node_of(first, self.me2)
+        weight, slot = self.wt[pl.ds(owner, 1), :], self.et[pl.ds(owner, 1), :]
+        sub, lane = iota((self.block, tall), 0), iota((self.block, tall), 1)
+        mine = (sub % self.seconds == lane // LANES) & (slot == (sub // self.seconds).astype(F32))
+        self.at[first] = jnp.where(mine, weight, 0.0).astype(BF16)
+
+    def spread(self, first, upper, lower):
+        key = self.key_row(first, upper, lower)
+        self.pt[first] = ones_where(iota((self.pt.shape[1], self.block), 0).astype(F32) == key)
+
+    def finish(self):
+        for stage in (self.tables, self.rows_out, self.sums_out, self.agg_out, self.rows_back):
+            stage.finish()
 
 
 class NodeSum:
@@ -300,23 +371,36 @@
 
 def tower_kernel(
     nodes, grps, nbr_ref, tgt_ref, msgw_ref, combw_ref, gain_ref, served_ref, owners_ref, weight_ref, labels_ref, pos_ref,
-    loss_ref, gmsg_ref, gcomb_ref, ghead_ref,
-    msg_ref, msg2_ref, bf_ref, slope_ref, serve_ref,
-    out_ref, in_ref, send_sem, recv_sem, a1_ref, a2_ref, at1_ref, at2_ref, front_ref, back_ref, comb_in_ref, pre_ref,
+    loss_ref, mfull, cfull,
+    msg0_ref, msg1_ref, bf_ref, slope_ref, upper_ref, lower_ref, path0, path1, sems0, sems1,
+    comb_in_ref, pre_ref,
     all_ref, query_ref, gains_ref, rt_ref, ct_ref, ring_send, ring_recv, stat_ref, stat_send, stat_recv,
-    out2_ref, in2_ref, send2_sem, recv2_sem, acc_ref, acc2_ref,
-    cpart_ref, cland_ref, cpart_send, cpart_recv, cpieces, cz_in, cmine, cy_in, cfull, c0, c1, c2, c3, c4, c5,
+    acc_ref,
+    cpart_ref, cland_ref, cpart_send, cpart_recv, cpieces, cz_in, cmine, cy_in, c0, c1, c2, c3, c4, c5,
     mpart_ref, pair_ref, pair_send, pair_recv, mhalf_ref, mland_ref, mx_send, mx_recv,
-    mpieces, mz_in, mmine, my_in, mfull, m0, m1, m2, m3, m4, m5,
+    mpieces, mz_in, mmine, my_in, m0, m1, m2, m3, m4, m5,
 ):
     ready = greet(nodes, grps)
     node, me = lax.axis_index("node"), lax.axis_index("grp")
     feat, tgts, pins = msgw_ref.shape[0], tgt_ref.shape[0], nbr_ref.shape[0]
-    half, planes, span, group = feat // 2, nodes // ROW, nodes * SPAN, tgts * grps
-    chunks = span // LANES
-    per = LANES // SPAN
+    half, group = feat // 2, tgts * grps
     lane = iota((LANES, LANES), 1)
     sub = iota((LANES, LANES), 0)
+    cap = served_ref.shape[0]
+    paths = [Path(nodes, True, cap, path0, sems0), Path(nodes, False, cap, path1, sems1)]
+    longest = max(path.firsts for path in paths)
+    halves = (msg0_ref, msg1_ref)
+
+    def each_first(first, act):
+        def turn(step, _):
+            for which, path in enumerate(paths):
+                if path.firsts == longest:
+                    act(path, which, step)
+                else:
+                    pl.when(step < path.firsts)(functools.partial(act, path, which, step))
+            return 0
+
+        lax.fori_loop(first, longest, turn, 0)
 
     def message(tile, _):
         at = rows(tile * LANES, LANES)
@@ -325,89 +409,57 @@
         pre = dot(nbr, msgw_ref[...])
         slope_ref[at, :] = pre
         msg = (pre * sigmoid(pre)).astype(BF16)
-        msg_ref[at, :] = msg
-        msg2_ref[at, :] = msg[:, :half]
-        msg2_ref[rows(pins + tile * LANES, LANES), :] = msg[:, half:]
+        msg0_ref[at, :] = msg[:, :half]
+        msg1_ref[at, :] = msg[:, half:]
         return 0
 
     lax.fori_loop(0, pins // LANES, message, 0)
-    serve_ref[...] = jnp.zeros_like(serve_ref)
-    serve_ref[: served_ref.shape[0], : served_ref.shape[1]] = served_ref[...]
-    forth = Exchange(nodes, out_ref, in_ref, send_sem, recv_sem)
-    back = Exchange(nodes, out2_ref, in2_ref, send2_sem, recv2_sem)
-
-    def keys_of(chunk, sign):
-        peers = forth.peer(sub // SPAN + chunk * per, sign)
-        pick = ones_where(lane == peers)
-        table = serve_ref[...]
-        upper = (table // 2).astype(F32).astype(BF16)
-        lower = (table % 2).astype(F32).astype(BF16)
-        listed = dot(pick, upper) * 2.0 + dot(pick, lower)
-        place = sub % SPAN
-        key1 = jnp.sum(jnp.where(lane == place, listed, 0.0), axis=1, keepdims=True)
-        key2 = jnp.sum(jnp.where(lane == FRONT + place % 8, listed, 0.0), axis=1, keepdims=True)
-        key1 = jnp.broadcast_to(key1, (LANES, LANES))
-        key2 = jnp.broadcast_to(key2, (LANES, LANES)) + jnp.where(place >= 8, float(pins), 0.0)
-        return key1.astype(I32), key2.astype(I32)
-
+    upper_ref[...] = jnp.zeros_like(upper_ref)
+    lower_ref[...] = jnp.zeros_like(lower_ref)
+    served = served_ref[...]
+    upper_ref[:cap, : served.shape[1]] = (served // 2).astype(F32)
+    lower_ref[:cap, : served.shape[1]] = (served % 2).astype(F32)
+    upper, lower = upper_ref[...].astype(BF16), lower_ref[...].astype(BF16)
+    for path in paths:
+        path.put_tables(owners_ref[...], weight_ref[...])
     ready()
-
-    def serve(chunk, _):
-        at = rows(chunk * LANES, LANES)
-        key1, key2 = keys_of(chunk, 1)
-        pick1 = jnp.concatenate([ones_where(key1 == lane + c * LANES) for c in range(pins // LANES)], 1)
-        pick2 = jnp.concatenate([ones_where(key2 == lane + c * LANES) for c in range(2 * pins // LANES)], 1)
-        out_ref[at, :feat] = dot(pick1, msg_ref[...]).astype(BF16)
-        out_ref[at, feat:] = dot(pick2, msg2_ref[...]).astype(BF16)
-        forth.start(jnp.maximum(chunk * per, 1), chunk * per + per)
-        return 0
-
-    lax.fori_loop(0, chunks, serve, 0)
-    forth.keep()
-
-    hits_t = jnp.zeros((LANES, tgts), F32)
-    weights_t = jnp.zeros((LANES, tgts), F32)
-    for k in range(owners_ref.shape[0]):
-        hit = owners_ref[k : k + 1, :] == sub
-        hits_t = hits_t + jnp.where(hit, 1.0, 0.0)
-        weights_t = weights_t + jnp.where(hit, weight_ref[k : k + 1, :].astype(F32), 0.0)
+    for path in paths:
+        path.tables.start()
+
+    def serve(path, which, step):
+        first = path.first(step)
+        path.serve(first, upper, lower, halves[which])
+        path.rows_out.copy(first, path.me1).start()
+
+    each_first(1, serve)
+    for path, messages in zip(paths, halves):
+        path.serve(path.me1, upper, lower, messages)
+        path.keep(path.out, path.inn)
+
     above = ones_where(sub < lane)
-    earlier_t = dot(hits_t.astype(BF16), above)
-    weights = jnp.transpose(weights_t)
-    total = jnp.sum(weights, axis=1, keepdims=True)
-    earlier = jnp.transpose(earlier_t).astype(BF16)
-    weights, earlier_t, weights_t = weights.astype(BF16), earlier_t.astype(BF16), weights_t.astype(BF16)
-
-    def weigh(chunk, _):
-        at = rows(chunk * LANES, LANES)
-        spread = ones_where(sub == forth.peer(lane // SPAN + chunk * per, -1))
-        slot, weight = dot(earlier, spread), dot(weights, spread)
-        place = lane % SPAN
-        a1_ref[:, at] = jnp.where(slot == place.astype(F32), weight, 0.0).astype(BF16)
-        late = jnp.where(slot == (FRONT + place % 8).astype(F32), weight, 0.0)
-        a2_ref[:tgts, at] = jnp.where(place < 8, late, 0.0).astype(BF16)
-        a2_ref[tgts:, at] = jnp.where(place >= 8, late, 0.0).astype(BF16)
-        spread = ones_where(lane == forth.peer(sub // SPAN + chunk * per, 1))
-        slot, weight = dot(spread, earlier_t), dot(spread, weights_t)
-        place = sub % SPAN
-        at1_ref[at, :] = jnp.where(slot == place.astype(F32), weight, 0.0).astype(BF16)
-        late = jnp.where(slot == (FRONT + place % 8).astype(F32), weight, 0.0)
-        at2_ref[at, :tgts] = jnp.where(place < 8, late, 0.0).astype(BF16)
-        at2_ref[at, tgts:] = jnp.where(place >= 8, late, 0.0).astype(BF16)
-        return 0
-
-    lax.fori_loop(0, chunks, weigh, 0)
-
+    for path in paths:
+        path.tables.arrive()
+        path.read_tables(above)
+    each_first(0, lambda path, which, step: path.weigh(path.first(step)))
+    for path in paths:
+        path.sums[...] = dot(path.a[path.me1], path.inn[rows(path.me1 * path.block, path.block), :])
+    own_path = paths[0]
+    total = jnp.sum(own_path.ws[rows(own_path.me2 * LANES, LANES), :].astype(F32), axis=1, keepdims=True)
     tgt_bf = tgt_ref[...].astype(BF16)
     comb_in_ref[:, :feat] = tgt_bf
     pre_ref[...] = dot(tgt_bf, combw_ref[:feat, :])
 
-    def slopes(tile, _):
-        at = rows(tile * LANES, LANES)
-        slope_ref[at, :] = silu_slope(slope_ref[at, :])
-        return 0
-
-    lax.fori_loop(0, pins // LANES, slopes, 0)
+    def collect(path, which, step):
+        first = path.first(step)
+        path.rows_out.copy(first, first).wait_recv()
+        path.sums[...] += dot(path.a[first], path.inn[rows(first * path.block, path.block), :])
+
+    each_first(1, collect)
+    for path in paths:
+        path.sent[...] = path.sums[...].astype(BF16)
+        path.sums_out.start()
+
+    each_first(0, lambda path, which, step: path.weigh_back(path.first(step)))
     gain = gain_ref[...]
     gain_hi = gain.astype(BF16).astype(F32)
     gain_mid = (gain - gain_hi).astype(BF16).astype(F32)
@@ -424,24 +476,13 @@
         return 0
 
     lax.fori_loop(0, grps, gains, 0)
-    front_ref[...] = jnp.zeros_like(front_ref)
-    back_ref[...] = jnp.zeros_like(back_ref)
-    acc_ref[...] = jnp.zeros_like(acc_ref)
-    acc2_ref[...] = jnp.zeros_like(acc2_ref)
-
-    def collect(chunk, _):
-        at = rows(chunk * LANES, LANES)
-        forth.arrive(jnp.maximum(chunk * per, 1), chunk * per + per)
-        front_ref[...] += dot(a1_ref[:, at], in_ref[at, :feat])
-        back_ref[...] += dot(a2_ref[:, at], in_ref[at, feat:])
-        return 0
-
-    lax.fori_loop(0, chunks, collect, 0)
-    aggregate = front_ref[...] + jnp.concatenate([back_ref[:tgts, :], back_ref[tgts:, :]], axis=1)
-    agg_bf = (aggregate / total).astype(BF16)
+    sums = []
+    for path in paths:
+        path.sums_out.arrive()
+        sums.append(path.sums_out.total(path.sums[rows(path.me2 * LANES, LANES), :]))
+    agg_bf = (jnp.concatenate(sums, axis=1) / total).astype(BF16)
     comb_in_ref[:, feat:] = agg_bf
     comb_pre = pre_ref[...] + dot(agg_bf, combw_ref[feat:, :])
-    pre_ref[...] = comb_pre
     hidden = comb_pre * sigmoid(comb_pre)
     inv_norm = lax.rsqrt(jnp.mean(hidden * hidden, axis=1, keepdims=True) + eps)
     embed = (hidden * inv_norm).astype(BF16)
@@ -510,21 +551,10 @@
     pre_grad = (slope * hidden_grad).astype(BF16)
     agg = dot_nt(pre_grad, combw_ref[feat:, :]) / total
 
-    agg_hi = agg.astype(BF16)
-    agg_lo = (agg - agg_hi.astype(F32)).astype(BF16)
-    both = jnp.concatenate([agg_hi, agg_lo], axis=0)
-    both2 = jnp.concatenate([halves_stacked(agg_hi), halves_stacked(agg_lo)], axis=0)
-
-    def give(chunk, _):
-        at = rows(chunk * LANES, LANES)
-        w1, w2 = at1_ref[at, :], at2_ref[at, :]
-        out2_ref[at, :feat] = dot(jnp.concatenate([w1, w1], axis=1), both).astype(BF16)
-        out2_ref[at, feat:] = dot(jnp.concatenate([w2, w2], axis=1), both2).astype(BF16)
-        back.start(jnp.maximum(chunk * per, 1), chunk * per + per)
-        return 0
-
-    lax.fori_loop(0, chunks, give, 0)
-    back.keep()
+    agg_bf = agg.astype(BF16)
+    for which, path in enumerate(paths):
+        path.agg[rows(path.me2 * LANES, LANES), :] = agg_bf[:, which * half : which * half + half]
+        path.agg_out.start()
 
     cols = feat // grps
     cpart_ref[:, : 2 * feat] = dot_tn(pre_grad, comb_in_ref[...]).astype(BF16)
@@ -540,24 +570,38 @@
     comb_full = NodeSum(nodes, cpieces, cz_in, cmine, cy_in, cfull, (c0, c1, c2, c3, c4, c5))
     msg_full = NodeSum(nodes, mpieces, mz_in, mmine, my_in, mfull, (m0, m1, m2, m3, m4, m5))
 
-    def take(chunk, _):
-        at = rows(chunk * LANES, LANES)
-        key1, key2 = keys_of(chunk, -1)
-        key1, key2 = jnp.transpose(key1), jnp.transpose(key2)
-        spread1 = jnp.concatenate([ones_where(key1 == sub + c * LANES) for c in range(pins // LANES)], 0)
-        spread2 = jnp.concatenate([ones_where(key2 == sub + c * LANES) for c in range(2 * pins // LANES)], 0)
-        back.arrive(jnp.maximum(chunk * per, 1), chunk * per + per)
-        acc_ref[...] += dot(spread1, in2_ref[at, :feat])
-        acc2_ref[...] += dot(spread2, in2_ref[at, feat:])
+    each_first(0, lambda path, which, step: path.spread(path.first(step), upper, lower))
+
+    for path in paths:
+        path.agg_out.arrive()
+
+    def give(path, which, step):
+        first = path.first(step)
+        path.out2[rows(first * path.block, path.block), :] = dot(path.at[first], path.agg[...]).astype(BF16)
+        path.rows_back.copy(first, path.me1).start()
+
+    each_first(1, give)
+
+    def slopes(tile, _):
+        at = rows(tile * LANES, LANES)
+        slope_ref[at, :] = silu_slope(slope_ref[at, :])
         return 0
 
-    lax.fori_loop(0, chunks - 2, take, 0)
-    comb_sum.arrive()
-    comb_full.begin(comb_sum.total(cpart_ref[rows(me * cols, cols), :].astype(F32)))
-    lax.fori_loop(chunks - 2, chunks, take, 0)
-
-    row_grad = acc_ref[...] + jnp.concatenate([acc2_ref[:pins, :], acc2_ref[pins:, :]], axis=1)
-    msg_grad = (slope_ref[...] * row_grad).astype(BF16)
+    lax.fori_loop(0, pins // LANES, slopes, 0)
+    for which, path in enumerate(paths):
+        kept = dot(path.at[path.me1], path.agg[...]).astype(BF16)
+        acc_ref[:, which * half : which * half + half] = dot(path.pt[path.me1], kept)
+
+    def take(path, which, step):
+        first = path.first(step)
+        path.rows_back.copy(first, first).wait_recv()
+        acc_ref[:, which * half : which * half + half] += dot(
+            path.pt[first], path.in2[rows(first * path.block, path.block), :]
+        )
+
+    each_first(1, take)
+
+    msg_grad = (slope_ref[...] * acc_ref[...]).astype(BF16)
     part = dot_tn(msg_grad, bf_ref[...]).astype(BF16)
     for g in range(grps):
         first = (g % 2) * half + (g // 2) * cols
@@ -572,36 +616,43 @@
         device_id_type=MESH,
     )
     pair.start()
-    comb_full.over_y()
+    comb_sum.arrive()
+    comb_full.begin(comb_sum.total(cpart_ref[rows(me * cols, cols), :].astype(F32)))
     pair.wait_recv()
     mhalf_ref[...] = (mpart_ref[rows(core * half, half), :].astype(F32) + pair_ref[...].astype(F32)).astype(BF16)
     over_x = Stage(
         grps // 2, chip, lambda to: (node, to * 2 + core), lambda to: mhalf_ref.at[rows(to * cols, cols), :], mland_ref, cols, mx_send, mx_recv
     )
     over_x.start()
-    comb_full.gather()
+    comb_full.over_y()
     over_x.arrive()
     msg_full.begin(over_x.total(mhalf_ref[rows(chip * cols, cols), :].astype(F32)))
-    comb_full.end()
-    comb_value = from_pieces(cfull, (cols, 2 * feat + LANES))
-    gcomb_ref[...] = comb_value[:, : 2 * feat]
-    head_value = comb_value[:, 2 * feat :]
-    if cols < LANES:
-        head_value = jnp.concatenate([head_value, jnp.zeros((LANES - cols, LANES), F32)], axis=0)
-    ghead_ref[...] = jnp.transpose(head_value)[:tasks, :]
+    comb_full.gather()
     msg_full.over_y()
     msg_full.gather()
-    forth.finish()
+    for path in paths:
+        path.finish()
     ring.finish()
     stats.finish()
-    back.finish()
     comb_sum.finish()
+    comb_full.end()
     comb_full.finish()
     pair.wait_send()
     over_x.finish()
     msg_full.end()
-    gmsg_ref[...] = from_pieces(mfull, (cols, feat))
     msg_full.finish()
+
+
+def outputs_kernel(loss_in, mfull, cfull, loss_ref, gmsg_ref, gcomb_ref, ghead_ref):
+    loss_ref[...] = loss_in[...]
+    gmsg_ref[...] = from_pieces(mfull, gmsg_ref.shape)
+    cols, both = gcomb_ref.shape
+    value = from_pieces(cfull, (cols, both + LANES))
+    gcomb_ref[...] = value[:, :both]
+    head = value[:, both:]
+    if cols < LANES:
+        head = jnp.concatenate([head, jnp.zeros((LANES - cols, LANES), F32)], axis=0)
+    ghead_ref[...] = jnp.transpose(head)[: ghead_ref.shape[0], : ghead_ref.shape[1]]
 
 
 def body(
@@ -610,11 +661,10 @@
 ):
     pins, feat = nbr_feats.shape
     tgts, tasks = tgt_feats.shape[0], head_gain.shape[0]
-    group, span, half = tgts * grps, nodes * SPAN, feat // 2
+    group, half = tgts * grps, feat // 2
     cols, planes, chips = feat // grps, nodes // ROW, grps // 2
-    hops = chips // 2
+    hops, cap = chips // 2, serve_rows.shape[2]
     links = 2 * max(2 * hops - 1, 0)
-    block = feat + half
     wide = 2 * feat + LANES
 
     def vm(kind, *shape):
@@ -623,30 +673,46 @@
     def dma(*shape):
         return pltpu.SemaphoreType.DMA(shape)
 
+    def per_of(width):
+        return -(-(cols // 8 * (width // LANES)) // planes) * LANES
+
     def sum_scratch(width):
-        per = -(-(cols // 8 * (width // LANES)) // planes) * LANES
-        piece = [vm(F32, planes * 8, per), vm(F32, planes * 8, per), vm(F32, 8, per), vm(F32, ROW * 8, per), vm(F32, planes * 8, per)]
+        per = per_of(width)
+        piece = [vm(F32, planes * 8, per), vm(F32, planes * 8, per), vm(F32, 8, per), vm(F32, ROW * 8, per)]
         return piece + [dma(planes), dma(planes), dma(ROW), dma(ROW), dma(planes), dma(planes)]
 
+    def path_scratch(firsts, seconds):
+        block, tall = cap * seconds, seconds * LANES
+        return [
+            vm(I32, seconds * 16, LANES), vm(BF16, tall, LANES), vm(BF16, tall, LANES), vm(F32, LANES, tall), vm(F32, LANES, tall),
+            vm(BF16, firsts, tall, block), vm(BF16, firsts, block, tall), vm(BF16, firsts, pins, block),
+            vm(BF16, firsts * block, half), vm(BF16, firsts * block, half),
+            vm(F32, tall, half), vm(BF16, tall, half), vm(BF16, tall, half), vm(BF16, tall, half),
+            vm(BF16, firsts * block, half), vm(BF16, firsts * block, half),
+        ]
+
+    def path_sems(firsts, seconds):
+        counts = [seconds, firsts, seconds, seconds, firsts]
+        return [dma(count) for count in counts for _ in range(2)]
+
     scratch = [
-        vm(BF16, pins, feat), vm(BF16, 2 * pins, half), vm(BF16, pins, feat), vm(F32, pins, feat), vm(I32, LANES, LANES),
-        vm(BF16, span, block), vm(BF16, span, block), dma(nodes), dma(nodes),
-        vm(BF16, tgts, span), vm(BF16, 2 * tgts, span), vm(BF16, span, tgts), vm(BF16, span, 2 * tgts),
-        vm(F32, tgts, feat), vm(F32, 2 * tgts, half), vm(BF16, tgts, 2 * feat), vm(F32, tgts, feat),
+        vm(BF16, pins, half), vm(BF16, pins, half), vm(BF16, pins, feat), vm(F32, pins, feat), vm(F32, LANES, LANES), vm(F32, LANES, LANES),
+        path_scratch(ROW, planes), path_scratch(planes, ROW), path_sems(ROW, planes), path_sems(planes, ROW),
+        vm(BF16, tgts, 2 * feat), vm(F32, tgts, feat),
         vm(BF16, group, feat), vm(BF16, group, feat), vm(F32, group, feat), vm(F32, group, tgts), vm(F32, group, tgts),
         dma(2 * links + 2), dma(2 * links + 2), vm(F32, grps * 8, LANES), dma(grps), dma(grps),
-        vm(BF16, span, block), vm(BF16, span, block), dma(nodes), dma(nodes), vm(F32, pins, feat), vm(F32, 2 * pins, half),
+        vm(F32, pins, feat),
         vm(BF16, feat, wide), vm(BF16, feat, wide), dma(grps), dma(grps), *sum_scratch(wide),
         vm(BF16, feat, feat), vm(BF16, half, feat), pltpu.SemaphoreType.DMA, pltpu.SemaphoreType.DMA,
         vm(BF16, half, feat), vm(BF16, half, feat), dma(chips), dma(chips), *sum_scratch(feat),
     ]
     args = (
-        nbr_feats, tgt_feats, msg_weight, comb_weight, head_gain, serve_rows[0], owners.T, importance.T,
+        nbr_feats, tgt_feats, msg_weight, comb_weight, head_gain, serve_rows[0].T, owners.T, importance.T,
         labels.reshape(grps, tgts), positives.reshape(grps, tgts),
     )
     whole = pl.BlockSpec(memory_space=pltpu.VMEM)
-    outs = [(1, tgts), (cols, feat), (cols, 2 * feat), (tasks, max(cols, LANES))]
-    loss, grad_msg, grad_comb, grad_head = pl.pallas_call(
+    outs = [(1, tgts), (planes * 8, per_of(feat)), (planes * 8, per_of(wide))]
+    sums = pl.pallas_call(
         functools.partial(tower_kernel, nodes, grps),
         name="tower",
         out_shape=[jax.ShapeDtypeStruct(shape, F32) for shape in outs],
@@ -657,7 +723,15 @@
             collective_id=0, has_side_effects=True, vmem_limit_bytes=60 * 2**20
         ),
     )(*args)
-    return loss.reshape(tgts), grad_msg.T, grad_comb.T, grad_head[:, :cols]
+    outs = [(1, tgts), (cols, feat), (cols, 2 * feat), (tasks, cols)]
+    loss, grad_msg, grad_comb, grad_head = pl.pallas_call(
+        outputs_kernel,
+        name="outputs",
+        out_shape=[jax.ShapeDtypeStruct(shape, F32) for shape in outs],
+        in_specs=[whole] * len(sums),
+        out_specs=[whole] * len(outs),
+    )(*sums)
+    return loss.reshape(tgts), grad_msg.T, grad_comb.T, grad_head
 
 
 def solution(mesh):

time: 172 us -> 161 us (0.936)
  the two profiles are of different devices: /device:TPU:4 before, /device:TPU:2 now
where the time goes in v2:
time: 161 us; the launch traced here: 160 us
  Pallas kernels  160 us (99%)
    pallas_call x1, Pallas kernels, body(): pl.pallas_call(functools.partial(tower_kernel, nodes, grps), name='tower'...  158 us

profile of v2, /device:TPU:2, one launch (start us, length us, event | category | flops | bytes accessed | tf_op | source)
XLA Modules:
  0.0 160.4 jit_solution(8733002428503196938)
XLA Ops:
  0.6 158.1 %tower.1 = (f32[1,128]{1,0:T(1,128)}, f32[64,256]{1,0:T(8,128)}, f32[64,640]{1,0:T(8,128)}) custom-call(f32[512,512]{1,0:T(8,128)} %nbr_ref.1, f32[128,512]{1,0:T(8,128)} %tgt_ref.1, bf16[512,512]{1,0:T(8,128)(2,1)} %msgw_ref.1, bf16[1024,512]{1,0:T(8,128)(2,1)} %combw_ref.1, f32[8,512]{1,0:T(8,128)} %gain_ref.1, s32[24,64]{1,0:T(8,128)} %bitcast.10, ...), custom_call_target="tpu_custom_call" | custom-call | tf_op jit(solution)/shard_map/tower/pallas_call | solution.py:715
  158.7 1.6 %outputs.1 = (f32[1,128]{1,0:T(1,128)}, f32[32,512]{1,0:T(8,128)}, f32[32,1024]{1,0:T(8,128)}, f32[8,32]{1,0:T(8,128)}) custom-call(f32[1,128]{1,0:T(1,128)} %get-tuple-element.11.loss_in, f32[64,256]{1,0:T(8,128)} %get-tuple-element.12.mfull, f32[64,640]{1,0:T(8,128)} %get-tuple-element.13.cfull), custom_call_target="tpu_custom_call" | custom-call | tf_op jit(solution)/shard_map/outputs/pallas_call | solution.py:727

commit v3 on v2

--- a/solution.py
+++ b/solution.py
@@ -32,6 +32,14 @@
 
 def ones_where(mask):
     return jnp.where(mask, 1.0, 0.0).astype(BF16)
+
+
+def low(index, count):
+    return index & (count - 1)
+
+
+def high(index, count):
+    return lax.shift_right_logical(index, jnp.full(index.shape, count.bit_length() - 1, I32))
 
 
 def sigmoid(value):
@@ -147,7 +155,7 @@
         self.me1, self.me2 = (y, z) if y_first else (z, y)
         self.block = cap * self.seconds
         (self.tab, self.ws, self.es, self.wt, self.et, self.a, self.at, self.pt, self.out, self.inn, self.sums, self.sent, self.land,
-         self.agg, self.out2, self.in2) = refs
+         self.agg, self.out2, self.in2, self.code) = refs
         block, me1, me2 = self.block, self.me1, self.me2
         firsts, seconds, peer1, peer2 = self.firsts, self.seconds, self.peer1, self.peer2
 
@@ -181,16 +189,16 @@
 
     def key_column(self, first, upper, lower):
         sub, lane = iota((self.block, LANES), 0), iota((self.block, LANES), 1)
-        pick = ones_where(lane == self.node_of(first, sub % self.seconds))
+        pick = ones_where(lane == self.node_of(first, low(sub, self.seconds)))
         listed = dot_nt(pick, upper) * 2.0 + dot_nt(pick, lower)
-        return jnp.sum(jnp.where(lane == sub // self.seconds, listed, 0.0), axis=1, keepdims=True)
+        return jnp.sum(jnp.where(lane == high(sub, self.seconds), listed, 0.0), axis=1, keepdims=True)
 
     def key_row(self, first, upper, lower):
         sub, lane = iota((self.block, LANES), 0), iota((self.block, LANES), 1)
-        pick = ones_where(lane == self.node_of(first, sub % self.seconds))
+        pick = ones_where(lane == self.node_of(first, low(sub, self.seconds)))
         listed = dot_nt(upper, pick) * 2.0 + dot_nt(lower, pick)
         sub, lane = iota((LANES, self.block), 0), iota((LANES, self.block), 1)
-        return jnp.sum(jnp.where(sub == lane // self.seconds, listed, 0.0), axis=0, keepdims=True)
+        return jnp.sum(jnp.where(sub == high(lane, self.seconds), listed, 0.0), axis=0, keepdims=True)
 
     def serve(self, first, upper, lower, messages):
         key = self.key_column(first, upper, lower)
@@ -222,21 +230,26 @@
         lax.fori_loop(0, self.seconds, read, 0)
 
     def weigh(self, first):
-        tall = self.seconds * LANES
         owner = self.node_of(first, self.me2)
         spread = ones_where(iota((LANES, self.block), 0) == owner)
         weight, slot = dot(self.ws[...], spread), dot(self.es[...], spread)
-        sub, lane = iota((tall, self.block), 0), iota((tall, self.block), 1)
-        mine = (lane % self.seconds == sub // LANES) & (slot == (lane // self.seconds).astype(F32))
-        self.a[first] = jnp.where(mine, weight, 0.0).astype(BF16)
+        lane = iota((8, self.block), 1)
+        for second in range(self.seconds):
+            at = slice(second * LANES, second * LANES + LANES)
+            code = jnp.where(low(lane, self.seconds) == second, high(lane, self.seconds), -1).astype(F32)[:1]
+            self.a[first, at, :] = jnp.where(slot[at] == code, weight[at], 0.0).astype(BF16)
+
+    def number(self):
+        sub = iota((self.block, LANES), 0)
+        for second in range(self.seconds):
+            self.code[second] = jnp.where(low(sub, self.seconds) == second, high(sub, self.seconds), -1).astype(F32)
 
     def weigh_back(self, first):
-        tall = self.seconds * LANES
         owner = self.node_of(first, self.me2)
         weight, slot = self.wt[pl.ds(owner, 1), :], self.et[pl.ds(owner, 1), :]
-        sub, lane = iota((self.block, tall), 0), iota((self.block, tall), 1)
-        mine = (sub % self.seconds == lane // LANES) & (slot == (sub // self.seconds).astype(F32))
-        self.at[first] = jnp.where(mine, weight, 0.0).astype(BF16)
+        for second in range(self.seconds):
+            at = slice(second * LANES, second * LANES + LANES)
+            self.at[first, :, at] = jnp.where(slot[:, at] == self.code[second], weight[:, at], 0.0).astype(BF16)
 
     def spread(self, first, upper, lower):
         key = self.key_row(first, upper, lower)
@@ -374,7 +387,7 @@
     loss_ref, mfull, cfull,
     msg0_ref, msg1_ref, bf_ref, slope_ref, upper_ref, lower_ref, path0, path1, sems0, sems1,
     comb_in_ref, pre_ref,
-    all_ref, query_ref, gains_ref, rt_ref, ct_ref, ring_send, ring_recv, stat_ref, stat_send, stat_recv,
+    all_ref, query_ref, gains_ref, rt_ref, ct_ref, gct_ref, ring_send, ring_recv, stat_ref, stat_send, stat_recv,
     acc_ref,
     cpart_ref, cland_ref, cpart_send, cpart_recv, cpieces, cz_in, cmine, cy_in, c0, c1, c2, c3, c4, c5,
     mpart_ref, pair_ref, pair_send, pair_recv, mhalf_ref, mland_ref, mx_send, mx_recv,
@@ -459,6 +472,8 @@
         path.sent[...] = path.sums[...].astype(BF16)
         path.sums_out.start()
 
+    for path in paths:
+        path.number()
     each_first(0, lambda path, which, step: path.weigh_back(path.first(step)))
     gain = gain_ref[...]
     gain_hi = gain.astype(BF16).astype(F32)
@@ -469,9 +484,11 @@
         [gain_hi, gain_mid, gain_lo, jnp.zeros((LANES - 3 * tasks, feat), F32)], axis=0
     ).astype(BF16)
 
+    task = lane % tasks
+
     def gains(block, _):
         label = as_column(labels_ref[pl.ds(block, 1), :])
-        pick = ones_where((label == lane % tasks) & (lane < 3 * tasks))
+        pick = ones_where((label == task) & (lane < 3 * tasks))
         gains_ref[rows(block * tgts, tgts), :] = dot(pick, gain3)
         return 0
 
@@ -499,8 +516,8 @@
         block_embed = all_ref[at, :]
         block_query = (block_embed.astype(F32) * gains_ref[at, :]).astype(BF16)
         query_ref[at, :] = block_query
-        rt_ref[at, :] = dot_nt(block_embed, own_query) / feat
-        ct_ref[at, :] = dot_nt(all_ref[own, :], block_query) / feat
+        rt_ref[at, :] = dot_nt(block_embed, own_query) * (1.0 / feat)
+        ct_ref[at, :] = dot_nt(all_ref[own, :], block_query) * (1.0 / feat)
 
     score(me)
     for hop in range(1, ring.hops + 1):
@@ -529,19 +546,21 @@
     hit = jnp.where(iota((group, tgts), 0) == pos_ref[pl.ds(me, 1), :], 1.0, 0.0)
     picked = jnp.sum(scores * hit, axis=0, keepdims=True)
     loss_ref[...] = top + jnp.log(norm) - picked
-    grad = ((terms / norm - hit) / group / feat).astype(BF16)
+    grad = ((terms * (1.0 / norm) - hit) * (1.0 / group / feat)).astype(BF16)
     query_grad = dot_tn(grad, all_ref[...])
     stats.arrive()
 
-    def column(block, acc):
-        at = rows(block * tgts, tgts)
+    place = sub + me * tgts
+
+    def column(block, _):
         stat = stat_ref[rows(block * 8, 8), :]
-        terms = jnp.exp(ct_ref[at, :] - stat[0:1, :]) / stat[4:5, :]
-        mine = iota((tgts, LANES), 0) + me * tgts == pos_ref[pl.ds(block, 1), :]
-        grad = ((terms - jnp.where(mine, 1.0, 0.0)) / group / feat).astype(BF16)
-        return acc + dot(grad, query_ref[at, :])
-
-    column_grad = lax.fori_loop(0, grps, column, jnp.zeros((tgts, feat), F32))
+        terms = jnp.exp(ct_ref[rows(block * tgts, tgts), :] - stat[0:1, :]) * (1.0 / stat[4:5, :])
+        hit = jnp.where(place == pos_ref[pl.ds(block, 1), :], 1.0, 0.0)
+        gct_ref[:, rows(block * tgts, tgts)] = ((terms - hit) * (1.0 / group / feat)).astype(BF16)
+        return 0
+
+    lax.fori_loop(0, grps, column, 0, unroll=4)
+    column_grad = dot(gct_ref[...], query_ref[...])
     embed_grad = query_grad * own_gain + column_grad
     logistic = sigmoid(comb_pre)
     inner = jnp.sum(hidden * embed_grad, axis=1, keepdims=True)
@@ -688,7 +707,7 @@
             vm(BF16, firsts, tall, block), vm(BF16, firsts, block, tall), vm(BF16, firsts, pins, block),
             vm(BF16, firsts * block, half), vm(BF16, firsts * block, half),
             vm(F32, tall, half), vm(BF16, tall, half), vm(BF16, tall, half), vm(BF16, tall, half),
-            vm(BF16, firsts * block, half), vm(BF16, firsts * block, half),
+            vm(BF16, firsts * block, half), vm(BF16, firsts * block, half), vm(F32, seconds, block, LANES),
         ]
 
     def path_sems(firsts, seconds):
@@ -699,7 +718,7 @@
         vm(BF16, pins, half), vm(BF16, pins, half), vm(BF16, pins, feat), vm(F32, pins, feat), vm(F32, LANES, LANES), vm(F32, LANES, LANES),
         path_scratch(ROW, planes), path_scratch(planes, ROW), path_sems(ROW, planes), path_sems(planes, ROW),
         vm(BF16, tgts, 2 * feat), vm(F32, tgts, feat),
-        vm(BF16, group, feat), vm(BF16, group, feat), vm(F32, group, feat), vm(F32, group, tgts), vm(F32, group, tgts),
+        vm(BF16, group, feat), vm(BF16, group, feat), vm(F32, group, feat), vm(F32, group, tgts), vm(F32, group, tgts), vm(BF16, tgts, group),
         dma(2 * links + 2), dma(2 * links + 2), vm(F32, grps * 8, LANES), dma(grps), dma(grps),
         vm(F32, pins, feat),
         vm(BF16, feat, wide), vm(BF16, feat, wide), dma(grps), dma(grps), *sum_scratch(wide),

time: 161 us -> 158 us (0.981)
  Pallas kernels: 160 us -> 157 us
    pallas_call x1, Pallas kernels: 158 us -> 156 us  [body(): pl.pallas_call(functools.partial(tower_kernel, nodes, grps), name='tower'...]
where the time goes in v3:
time: 158 us
  Pallas kernels  157 us (99%)
    pallas_call x1, Pallas kernels, body(): pl.pallas_call(functools.partial(tower_kernel, nodes, grps), name='tower'...  156 us

profile of v3, /device:TPU:2, one launch (start us, length us, event | category | flops | bytes accessed | tf_op | source)
XLA Modules:
  0.0 158.0 jit_solution(16395554203031301541)
XLA Ops:
  0.6 155.7 %tower.1 = (f32[1,128]{1,0:T(1,128)}, f32[64,256]{1,0:T(8,128)}, f32[64,640]{1,0:T(8,128)}) custom-call(f32[512,512]{1,0:T(8,128)} %nbr_ref.1, f32[128,512]{1,0:T(8,128)} %tgt_ref.1, bf16[512,512]{1,0:T(8,128)(2,1)} %msgw_ref.1, bf16[1024,512]{1,0:T(8,128)(2,1)} %combw_ref.1, f32[8,512]{1,0:T(8,128)} %gain_ref.1, s32[24,64]{1,0:T(8,128)} %bitcast.10, ...), custom_call_target="tpu_custom_call" | custom-call | tf_op jit(solution)/shard_map/tower/pallas_call | solution.py:734
  156.4 1.6 %outputs.1 = (f32[1,128]{1,0:T(1,128)}, f32[32,512]{1,0:T(8,128)}, f32[32,1024]{1,0:T(8,128)}, f32[8,32]{1,0:T(8,128)}) custom-call(f32[1,128]{1,0:T(1,128)} %get-tuple-element.11.loss_in, f32[64,256]{1,0:T(8,128)} %get-tuple-element.12.mfull, f32[64,640]{1,0:T(8,128)} %get-tuple-element.13.cfull), custom_call_target="tpu_custom_call" | custom-call | tf_op jit(solution)/shard_map/outputs/pallas_call | solution.py:746

commit v4 on v3

--- a/solution.py
+++ b/solution.py
@@ -106,6 +106,9 @@
 
     def start(self):
         self.each(lambda to: self.copy(to, self.me).start())
+
+    def start_step(self, step):
+        self.copy(lax.rem(self.me + offset(step, self.count), self.count), self.me).start()
 
     def arrive(self):
         self.each(lambda source: self.copy(source, source).wait_recv())
@@ -143,6 +146,20 @@
             band.append(ref[piece * 8 : piece * 8 + 8, place * LANES : place * LANES + LANES])
         bands.append(jnp.concatenate(band, axis=1))
     return jnp.concatenate(bands, axis=0)
+
+
+def start_together(stages):
+    longest = max(stage.count for stage in stages)
+
+    def turn(step, _):
+        for stage in stages:
+            if stage.count == longest:
+                stage.start_step(step)
+            else:
+                pl.when(step < stage.count)(functools.partial(stage.start_step, step))
+        return 0
+
+    lax.fori_loop(1, longest, turn, 0)
 
 
 class Path:
@@ -470,7 +487,7 @@
     each_first(1, collect)
     for path in paths:
         path.sent[...] = path.sums[...].astype(BF16)
-        path.sums_out.start()
+    start_together([path.sums_out for path in paths])
 
     for path in paths:
         path.number()
@@ -573,7 +590,7 @@
     agg_bf = agg.astype(BF16)
     for which, path in enumerate(paths):
         path.agg[rows(path.me2 * LANES, LANES), :] = agg_bf[:, which * half : which * half + half]
-        path.agg_out.start()
+    start_together([path.agg_out for path in paths])
 
     cols = feat // grps
     cpart_ref[:, : 2 * feat] = dot_tn(pre_grad, comb_in_ref[...]).astype(BF16)
@@ -585,7 +602,8 @@
     comb_sum = Stage(
         grps, me, lambda to: (node, to), lambda to: cpart_ref.at[rows(to * cols, cols), :], cland_ref, cols, cpart_send, cpart_recv
     )
-    comb_sum.start()
+    early = min(5, grps)
+    lax.fori_loop(1, early, lambda step, _: (comb_sum.start_step(step), 0)[1], 0)
     comb_full = NodeSum(nodes, cpieces, cz_in, cmine, cy_in, cfull, (c0, c1, c2, c3, c4, c5))
     msg_full = NodeSum(nodes, mpieces, mz_in, mmine, my_in, mfull, (m0, m1, m2, m3, m4, m5))
 
@@ -598,6 +616,12 @@
         first = path.first(step)
         path.out2[rows(first * path.block, path.block), :] = dot(path.at[first], path.agg[...]).astype(BF16)
         path.rows_back.copy(first, path.me1).start()
+        index = step + (4 if which == 0 else 11)
+        limit = min(grps, 12 if which == 0 else 16)
+
+        @pl.when(index < limit)
+        def _():
+            comb_sum.start_step(index)
 
     each_first(1, give)
 

time: 158 us -> 159 us (level)
  no operation moved by 1% of the time
where the time goes in v4:
time: 159 us
  Pallas kernels  158 us (99%)
    pallas_call x1, Pallas kernels, body(): pl.pallas_call(functools.partial(tower_kernel, nodes, grps), name='tower'...  157 us

profile of v4, /device:TPU:2, one launch (start us, length us, event | category | flops | bytes accessed | tf_op | source)
XLA Modules:
  0.0 158.9 jit_solution(13031569194916302444)
XLA Ops:
  0.6 156.6 %tower.1 = (f32[1,128]{1,0:T(1,128)}, f32[64,256]{1,0:T(8,128)}, f32[64,640]{1,0:T(8,128)}) custom-call(f32[512,512]{1,0:T(8,128)} %nbr_ref.1, f32[128,512]{1,0:T(8,128)} %tgt_ref.1, bf16[512,512]{1,0:T(8,128)(2,1)} %msgw_ref.1, bf16[1024,512]{1,0:T(8,128)(2,1)} %combw_ref.1, f32[8,512]{1,0:T(8,128)} %gain_ref.1, s32[24,64]{1,0:T(8,128)} %bitcast.10, ...), custom_call_target="tpu_custom_call" | custom-call | tf_op jit(solution)/shard_map/tower/pallas_call | solution.py:758
  157.2 1.6 %outputs.1 = (f32[1,128]{1,0:T(1,128)}, f32[32,512]{1,0:T(8,128)}, f32[32,1024]{1,0:T(8,128)}, f32[8,32]{1,0:T(8,128)}) custom-call(f32[1,128]{1,0:T(1,128)} %get-tuple-element.11.loss_in, f32[64,256]{1,0:T(8,128)} %get-tuple-element.12.mfull, f32[64,640]{1,0:T(8,128)} %get-tuple-element.13.cfull), custom_call_target="tpu_custom_call" | custom-call | tf_op jit(solution)/shard_map/outputs/pallas_call | solution.py:770
